TPU v7x, 256 devices: a whole 4x4x8 slice. The times are simulated.
256 devices in a mesh: sec: 2 (over z_hi), rcv: 128 (over y, z_lo, x, core).
Axes of the slice: x: 4, y: 4, z: 8 (z_hi: 2, z_lo: 4; z = z_hi * 4 + z_lo), core: 2. Of those that a mesh axis runs over, the one named last changes fastest.
Arguments:
- strain: float32 [16384, 8192], P('rcv', 'sec'), may hold values from -6 to 6
- offset: int32 [16384], P('rcv'), may hold values from 0 to 3
- fir_taps: float32 [64], replicated, may hold values from -0.75 to 0.75
- source_channel: int32 [256], P('rcv'), may hold values from 0 to 127
Outputs:
- correlations: bfloat16 [2, 128, 16384, 128], P('sec', None, 'rcv')
All inputs are finite; a program needn't handle non-finite values.
Results may differ from a plain program's by a relative error of at most 0.0068.
Values may be sent and summed in bfloat16 or wider, within the bound.
No kernel may reach another device: no remote copies, remote signals or barrier semaphores. Data moves between devices by JAX's collectives and lax.ppermute only.
A program may use at most 128 MiB of HBM per device.

v0:
```python
import math

import jax
import jax.numpy as jnp
from jax import lax
from jax.sharding import PartitionSpec as P

SRC_DEV = 2
TD = 2048
STRIDE = 4
TAPS = 64
BAND = 64
LAGS = 128
FREQ = 1024


def from_behind(array, axis, by):
    size = lax.axis_size(axis)
    pairs = [(i, i + by) for i in range(size) if 0 <= i + by < size]
    return lax.ppermute(array, axis, pairs)


def fir_weights(fir_taps, offset):
    shift_count = TAPS // STRIDE + 1
    phases = jnp.arange(STRIDE, dtype=jnp.int32)
    shifts = jnp.arange(shift_count, dtype=jnp.int32)
    tap_index = (
        TAPS + phases[:, None, None] - STRIDE * shifts[None, :, None] - phases[None, None, :]
    )
    matches = (tap_index[..., None] == jnp.arange(TAPS, dtype=jnp.int32)).astype(jnp.float32)
    per_phase = jnp.sum(matches * fir_taps, axis=-1)
    selector = (offset[:, None] == phases[None, :]).astype(jnp.float32)
    return jnp.einsum("co,oms->cms", selector, per_phase, precision=lax.Precision.HIGHEST)


def decimate(extended, weights, samples):
    channels = extended.shape[0]
    frames = extended.reshape(channels, -1, STRIDE).transpose(0, 2, 1)
    filtered = jnp.zeros((channels, samples), jnp.float32)
    for shift_pos in range(weights.shape[1]):
        for phase in range(STRIDE):
            filtered = (
                filtered
                + weights[:, shift_pos, phase, None]
                * frames[:, phase, shift_pos : shift_pos + samples]
            )
    return filtered


def row_parts(row_ids, first_half):
    half_bins = FREQ // 2
    half_id = first_half + row_ids // FREQ
    component = row_ids % FREQ // half_bins
    freq_id = half_id * half_bins + row_ids % half_bins
    return (component, freq_id)


def spectrum_block(row_ids, time_ids, traces):
    component, freq_id = row_parts(row_ids, 0)
    phase_ids = freq_id[:, None] * time_ids[None, :] % TD
    angles = 2.0 * math.pi / TD * phase_ids.astype(jnp.float32)
    dft_table = jnp.where(component[:, None] == 0, jnp.cos(angles), -jnp.sin(angles))
    return lax.dot_general(
        dft_table,
        traces,
        (((1,), (1,)), ((), ())),
        precision=lax.Precision.HIGHEST,
        preferred_element_type=jnp.float32,
    )


def whiten(spectra):
    halves = spectra.shape[0] // FREQ
    channels = spectra.shape[1]
    shaped = spectra.reshape(halves, 2, FREQ // 2 // BAND, BAND, channels)
    band_power = jnp.mean(shaped * shaped, axis=(1, 3), keepdims=True)
    return (shaped / jnp.sqrt(band_power + 1e-06)).reshape(spectra.shape).astype(jnp.bfloat16)


def lag_table(row_ids, first_half):
    component, freq_id = row_parts(row_ids, first_half)
    lag_ids = jnp.arange(LAGS, dtype=jnp.int32) - LAGS // 2
    phase_ids = freq_id[:, None] * lag_ids[None, :] % TD
    angles = 2.0 * math.pi / TD * phase_ids.astype(jnp.float32)
    return jnp.where(component[:, None] == 0, jnp.cos(angles), -jnp.sin(angles)).astype(
        jnp.bfloat16
    )


def select(white, local_ids):
    channels = white.shape[1]
    onehot = (local_ids[:, None] == jnp.arange(channels, dtype=jnp.int32)[None, :]).astype(
        jnp.bfloat16
    )
    return lax.dot_general(
        onehot, white, (((1,), (1,)), ((), ())), preferred_element_type=jnp.float32
    ).astype(jnp.bfloat16)


def cross_block(sources, receivers):
    block_size, row_count = sources.shape
    channels = receivers.shape[1]
    halves = row_count // FREQ
    half_bins = FREQ // 2
    source = sources.reshape(block_size, halves, 2, half_bins).astype(jnp.float32)
    receiver = receivers.reshape(halves, 2, half_bins, channels).astype(jnp.float32)
    cross_re = (
        source[:, :, 0, :, None] * receiver[None, :, 0]
        + source[:, :, 1, :, None] * receiver[None, :, 1]
    )
    cross_im = (
        source[:, :, 0, :, None] * receiver[None, :, 1]
        - source[:, :, 1, :, None] * receiver[None, :, 0]
    )
    return (
        jnp.stack([cross_re, cross_im], axis=2)
        .reshape(block_size, row_count, channels)
        .astype(jnp.bfloat16)
    )


def correlate(chosen, receivers, table):
    slot_count, block_count, row_count = chosen.shape
    source_count = slot_count * block_count
    block_size = math.gcd(source_count, 16)
    grouped = chosen.reshape(source_count // block_size, block_size, row_count)

    def per_block(sources):
        cross = cross_block(sources, receivers)
        return jnp.einsum("bfc,ft->bct", cross, table, preferred_element_type=jnp.float32)

    result = lax.map(per_block, grouped)
    return result.reshape(slot_count, block_count, receivers.shape[1], table.shape[1])


def per_device(strain, offset, fir_taps, source_channel):
    half_len = strain.shape[1]
    samples = half_len // STRIDE
    sec_pos = lax.axis_index("sec")
    left_rim = from_behind(strain[:, half_len - TAPS :], "sec", 1)
    decimated = decimate(
        jnp.concatenate([left_rim, strain], axis=1), fir_weights(fir_taps, offset), samples
    )
    time_ids = sec_pos * samples + jnp.arange(samples, dtype=jnp.int32)
    norm_scale = FREQ ** (-0.5)
    white_half = whiten(
        lax.psum_scatter(
            spectrum_block(
                jnp.arange(FREQ * lax.axis_size("sec"), dtype=jnp.int32), time_ids, decimated
            ),
            "sec",
            scatter_dimension=0,
            tiled=True,
        )
    )
    white_all = lax.all_gather(white_half, "sec", axis=0, tiled=True)
    half_slots = SRC_DEV // 2
    own_slots = lax.dynamic_slice_in_dim(source_channel, sec_pos * half_slots, half_slots)
    chosen = select(white_all, own_slots)[:, None, :]
    table = lag_table(jnp.arange(TD, dtype=jnp.int32), 0)
    partial_sums = correlate(lax.all_gather(chosen, "rcv", axis=1, tiled=True), white_all, table)
    return (partial_sums * norm_scale).astype(jnp.bfloat16)


def solution(mesh):
    in_specs = (P("rcv", "sec"), P("rcv"), P(), P("rcv"))
    out_specs = P("sec", None, "rcv", None)
    return jax.shard_map(
        per_device, mesh=mesh, in_specs=in_specs, out_specs=out_specs, check_vma=False
    )
```

profile of v0, /device:TPU:1, one launch (start us, length us, event | category | flops | bytes accessed | tf_op | source)
XLA Modules:
  0.0 888.1 jit_solution(4082071412543628077)
XLA Ops:
  6.5 1.9 copy.221
  8.5 9.6 %collective-permute-start = (f32[128,64]{0,1:T(8,128)S(1)}, f32[128,64]{0,1:T(8,128)S(1)}, u32[]{:S(2)}, u32[]{:S(2)}) collective-permute-start(f32[128,64]{0,1:T(8,128)S(1)} %slice.573), channel_id=1, source_target_pairs={{0,128},{1,129},{2,130},{3,131},{4,132},{5,133},{6,134},{7,135},{8... | collective-permute-start | bytes 98312 | tf_op jit(solution)/shard_map/ppermute | solution.py:20
  18.3 0.9 select_reduce_fusion
  19.3 0.9 fusion.259
  20.2 0.7 slice_bitcast_fusion.69
  20.9 0.7 slice_bitcast_fusion.68
  21.5 0.7 slice_bitcast_fusion.67
  22.2 0.6 slice_bitcast_fusion.66
  23.0 8.5 fusion.272
  31.6 9.1 %fusion.274 = (f32[128,1,1024]{0,1,2:T(1,128)S(1)}, f32[128,1,1024]{0,1,2:T(1,128)S(1)}, f32[128,1,1024]{0,1,2:T(1,128)S(1)}, f32[128,1,1024]{0,1,2:T(1,128)S(1)...) fusion(f32[128,4,1040]{0,1,2:T(4,128)S(1)} %bitcast.389), kind=kLoop, calls=%fused_computation.382 | loop fusion | bytes 19922944 | tf_op jit(solution)/shard_map/slice | solution.py:45
  40.6 9.5 %fusion.273 = (f32[128,1,1024]{0,1,2:T(1,128)}, f32[128,1,1024]{0,1,2:T(1,128)}, f32[128,1,1024]{0,1,2:T(1,128)}, f32[128,1,1024]{0,1,2:T(1,128)}, f32[128,1,102...) fusion(f32[128,4,1040]{0,1,2:T(4,128)S(1)} %bitcast.390), kind=kLoop, calls=%fused_computation.381 | loop fusion | bytes 19922944 | tf_op jit(solution)/shard_map/slice | solution.py:45
  50.1 6.5 fusion.275
  56.6 8.9 fusion.285
  65.5 44.1 %fusion.22 = f32[2048,128]{1,0:T(8,128)} fusion(s32[1024]{0:T(1024)S(1)} %iota_add_fusion, s32[2048]{0:T(1024)S(1)} %fusion.249, pred[2048]{0:T(1024)(128)(4,1)S(1)} %fusion.247, f32[128,1024]{0,1:T(8,128)} %fusion.285), kind=kOutput, calls=%fused_computation.41 | convolution fusion | flops 3254779904 | bytes 1587200 | tf_op jit(solution)/shard_map/dot_general | solution.py:63
  109.6 0.6 dynamic_slice.7
  110.2 39.6 %reduce-scatter.2.cloned.1.call-done = f32[1024,128]{1,0:T(8,128)} async-done(((f32[2048,128]{1,0:T(8,128)}), f32[1024,128]{1,0:T(8,128)}) %reduce-scatter.2.cloned.1.call-update) | async-done | bytes 524304 | tf_op jit(solution)/shard_map/reduce_scatter | solution.py:147
  149.8 1.3 mul.1070
  151.1 1.1 fusion.38
  152.2 14.1 %all_gather.6 = bf16[2048,128]{1,0:T(8,128)(2,1)S(1)} all-gather(bf16[1024,128]{1,0:T(8,128)(2,1)S(1)} %fusion.38), channel_id=1, replica_groups=mesh['sec'=2,'rcv'=128] {'sec'}, dimensions={0}, use_global_device_ids=true | all-gather | bytes 786432 | tf_op jit(solution)/shard_map/all_gather | solution.py:156
  166.3 0.8 fusion.261
  167.1 187.3 %all-gather = bf16[262144]{0:T(1024)(128)(2,1)S(1)} all-gather(bf16[2048]{0:T(1024)(128)(2,1)S(1)} %convert_element_type.51), channel_id=2, replica_groups=mesh['sec'=2,'rcv'=128] {'rcv'}, dimensions={0}, use_global_device_ids=true | all-gather | bytes 528384 | tf_op jit(solution)/shard_map/all_gather | solution.py:161
  354.6 520.1 %while.11 = (s32[]{:T(128)}, f32[8,16,128,128]{3,2,1,0:T(8,128)}, bf16[8,16,2048]{2,1,0:T(8,128)(2,1)S(1)}, bf16[2048,128]{1,0:T(8,128)(2,1)S(1)}, s32[128]{0:T(...) while((s32[]{:T(128)}, f32[8,16,128,128]{3,2,1,0:T(8,128)}, ...), condition=%wide.region_4.5_spmd.clone, body=%wide.region_3.4_spmd.clone.sunk | while | flops 1112047616 | bytes 59321432 | solution.py:132
  355.1 0.2 copy.366
  355.3 0.2 copy.367
  355.5 17.8 %add_convert_fusion.2 = (bf16[16,2,1,512,128]{3,2,1,4,0:T(2,128)(2,1)S(1)}, bf16[16,2,1,512,128]{3,2,1,4,0:T(2,128)(2,1)S(1)}) fusion(f32[2,512,128]{1,0,2:T(2,128)S(1)} %copy.366, f32[16,2,512]{2,1,0:T(2,128)S(1)} %get-tuple-element.264, f32[2,512,128]{1,0,2:T(2,128)S(1)} %copy.367, f32[16,2,512]{2,1,0:T(2,128)S(1)} %get-tuple-element.266), kind=kLoop, calls=%fused_computation.3.clone.1 | loop fusion | flops 16777216 | bytes 9568256 | tf_op jit(solution)/shard_map/convert.2
  373.4 20.3 %pad_maximum_fusion.3 = bf16[16,2,2,512,128]{3,2,1,4,0:T(2,128)(2,1)} fusion(bf16[16,2,1,512,128]{3,2,1,4,0:T(2,128)(2,1)S(1)} %get-tuple-element.267, bf16[16,2,1,512,128]{3,2,1,4,0:T(2,128)(2,1)S(1)} %get-tuple-element.268), kind=kLoop, calls=%fused_computation.1.clone.1 | loop fusion | flops 16777216 | bytes 16777216 | tf_op jit(solution)/shard_map/while/body/eval_jaxpr/stack | solution.py:116
  393.7 14.5 %convert_element_type.104 = bf16[16,2048,128]{1,2,0:T(8,128)(2,1)} reshape(bf16[16,2,2,512,128]{3,2,1,4,0:T(2,128)(2,1)} %pad_maximum_fusion.3) | data formatting | bytes 16777216 | tf_op jit(solution)/shard_map/while/body/eval_jaxpr/convert_element_type | solution.py:118
  408.2 11.4 %fusion.294 = f32[8,16,128,128]{3,2,1,0:T(8,128)} fusion(f32[8,16,128,128]{3,2,1,0:T(8,128)} %get-tuple-element.278, s32[]{:T(128)} %get-tuple-element.277, bf16[16,2048,128]{1,2,0:T(8,128)(2,1)} %convert_element_type.104, s32[128]{0:T(128)S(1)} %get-tuple-element.289, s32[2048]{0:T(1024)S(1)} %get-tuple-element.290, ...), kind=kOutput, calls=%fused_computation.10.clone.1 | convolution fusion | flops 1078198272 | bytes 9448448 | tf_op jit(solution)/shard_map/while/body/eval_jaxpr/bfc,ft->bct/dot_general | solution.py:130
  420.1 0.2 copy.366
  420.5 17.8 %add_convert_fusion.2 = (bf16[16,2,1,512,128]{3,2,1,4,0:T(2,128)(2,1)S(1)}, bf16[16,2,1,512,128]{3,2,1,4,0:T(2,128)(2,1)S(1)}) fusion(f32[2,512,128]{1,0,2:T(2,128)S(1)} %copy.366, f32[16,2,512]{2,1,0:T(2,128)S(1)} %get-tuple-element.264, f32[2,512,128]{1,0,2:T(2,128)S(1)} %copy.367, f32[16,2,512]{2,1,0:T(2,128)S(1)} %get-tuple-element.266), kind=kLoop, calls=%fused_computation.3.clone.1 | loop fusion | flops 16777216 | bytes 9568256 | tf_op jit(solution)/shard_map/convert.2
  438.4 20.3 %pad_maximum_fusion.3 = bf16[16,2,2,512,128]{3,2,1,4,0:T(2,128)(2,1)} fusion(bf16[16,2,1,512,128]{3,2,1,4,0:T(2,128)(2,1)S(1)} %get-tuple-element.267, bf16[16,2,1,512,128]{3,2,1,4,0:T(2,128)(2,1)S(1)} %get-tuple-element.268), kind=kLoop, calls=%fused_computation.1.clone.1 | loop fusion | flops 16777216 | bytes 16777216 | tf_op jit(solution)/shard_map/while/body/eval_jaxpr/stack | solution.py:116
  458.7 14.5 %convert_element_type.104 = bf16[16,2048,128]{1,2,0:T(8,128)(2,1)} reshape(bf16[16,2,2,512,128]{3,2,1,4,0:T(2,128)(2,1)} %pad_maximum_fusion.3) | data formatting | bytes 16777216 | tf_op jit(solution)/shard_map/while/body/eval_jaxpr/convert_element_type | solution.py:118
  473.2 11.4 %fusion.294 = f32[8,16,128,128]{3,2,1,0:T(8,128)} fusion(f32[8,16,128,128]{3,2,1,0:T(8,128)} %get-tuple-element.278, s32[]{:T(128)} %get-tuple-element.277, bf16[16,2048,128]{1,2,0:T(8,128)(2,1)} %convert_element_type.104, s32[128]{0:T(128)S(1)} %get-tuple-element.289, s32[2048]{0:T(1024)S(1)} %get-tuple-element.290, ...), kind=kOutput, calls=%fused_computation.10.clone.1 | convolution fusion | flops 1078198272 | bytes 9448448 | tf_op jit(solution)/shard_map/while/body/eval_jaxpr/bfc,ft->bct/dot_general | solution.py:130
  485.6 17.8 %add_convert_fusion.2 = (bf16[16,2,1,512,128]{3,2,1,4,0:T(2,128)(2,1)S(1)}, bf16[16,2,1,512,128]{3,2,1,4,0:T(2,128)(2,1)S(1)}) fusion(f32[2,512,128]{1,0,2:T(2,128)S(1)} %copy.366, f32[16,2,512]{2,1,0:T(2,128)S(1)} %get-tuple-element.264, f32[2,512,128]{1,0,2:T(2,128)S(1)} %copy.367, f32[16,2,512]{2,1,0:T(2,128)S(1)} %get-tuple-element.266), kind=kLoop, calls=%fused_computation.3.clone.1 | loop fusion | flops 16777216 | bytes 9568256 | tf_op jit(solution)/shard_map/convert.2
  503.5 20.3 %pad_maximum_fusion.3 = bf16[16,2,2,512,128]{3,2,1,4,0:T(2,128)(2,1)} fusion(bf16[16,2,1,512,128]{3,2,1,4,0:T(2,128)(2,1)S(1)} %get-tuple-element.267, bf16[16,2,1,512,128]{3,2,1,4,0:T(2,128)(2,1)S(1)} %get-tuple-element.268), kind=kLoop, calls=%fused_computation.1.clone.1 | loop fusion | flops 16777216 | bytes 16777216 | tf_op jit(solution)/shard_map/while/body/eval_jaxpr/stack | solution.py:116
  523.8 14.5 %convert_element_type.104 = bf16[16,2048,128]{1,2,0:T(8,128)(2,1)} reshape(bf16[16,2,2,512,128]{3,2,1,4,0:T(2,128)(2,1)} %pad_maximum_fusion.3) | data formatting | bytes 16777216 | tf_op jit(solution)/shard_map/while/body/eval_jaxpr/convert_element_type | solution.py:118
  538.3 11.4 %fusion.294 = f32[8,16,128,128]{3,2,1,0:T(8,128)} fusion(f32[8,16,128,128]{3,2,1,0:T(8,128)} %get-tuple-element.278, s32[]{:T(128)} %get-tuple-element.277, bf16[16,2048,128]{1,2,0:T(8,128)(2,1)} %convert_element_type.104, s32[128]{0:T(128)S(1)} %get-tuple-element.289, s32[2048]{0:T(1024)S(1)} %get-tuple-element.290, ...), kind=kOutput, calls=%fused_computation.10.clone.1 | convolution fusion | flops 1078198272 | bytes 9448448 | tf_op jit(solution)/shard_map/while/body/eval_jaxpr/bfc,ft->bct/dot_general | solution.py:130
  550.6 17.8 %add_convert_fusion.2 = (bf16[16,2,1,512,128]{3,2,1,4,0:T(2,128)(2,1)S(1)}, bf16[16,2,1,512,128]{3,2,1,4,0:T(2,128)(2,1)S(1)}) fusion(f32[2,512,128]{1,0,2:T(2,128)S(1)} %copy.366, f32[16,2,512]{2,1,0:T(2,128)S(1)} %get-tuple-element.264, f32[2,512,128]{1,0,2:T(2,128)S(1)} %copy.367, f32[16,2,512]{2,1,0:T(2,128)S(1)} %get-tuple-element.266), kind=kLoop, calls=%fused_computation.3.clone.1 | loop fusion | flops 16777216 | bytes 9568256 | tf_op jit(solution)/shard_map/convert.2
  568.5 20.3 %pad_maximum_fusion.3 = bf16[16,2,2,512,128]{3,2,1,4,0:T(2,128)(2,1)} fusion(bf16[16,2,1,512,128]{3,2,1,4,0:T(2,128)(2,1)S(1)} %get-tuple-element.267, bf16[16,2,1,512,128]{3,2,1,4,0:T(2,128)(2,1)S(1)} %get-tuple-element.268), kind=kLoop, calls=%fused_computation.1.clone.1 | loop fusion | flops 16777216 | bytes 16777216 | tf_op jit(solution)/shard_map/while/body/eval_jaxpr/stack | solution.py:116
  588.8 14.5 %convert_element_type.104 = bf16[16,2048,128]{1,2,0:T(8,128)(2,1)} reshape(bf16[16,2,2,512,128]{3,2,1,4,0:T(2,128)(2,1)} %pad_maximum_fusion.3) | data formatting | bytes 16777216 | tf_op jit(solution)/shard_map/while/body/eval_jaxpr/convert_element_type | solution.py:118
  603.3 11.4 %fusion.294 = f32[8,16,128,128]{3,2,1,0:T(8,128)} fusion(f32[8,16,128,128]{3,2,1,0:T(8,128)} %get-tuple-element.278, s32[]{:T(128)} %get-tuple-element.277, bf16[16,2048,128]{1,2,0:T(8,128)(2,1)} %convert_element_type.104, s32[128]{0:T(128)S(1)} %get-tuple-element.289, s32[2048]{0:T(1024)S(1)} %get-tuple-element.290, ...), kind=kOutput, calls=%fused_computation.10.clone.1 | convolution fusion | flops 1078198272 | bytes 9448448 | tf_op jit(solution)/shard_map/while/body/eval_jaxpr/bfc,ft->bct/dot_general | solution.py:130
  615.1 0.2 copy.366
  615.4 0.2 copy.367
  615.6 17.8 %add_convert_fusion.2 = (bf16[16,2,1,512,128]{3,2,1,4,0:T(2,128)(2,1)S(1)}, bf16[16,2,1,512,128]{3,2,1,4,0:T(2,128)(2,1)S(1)}) fusion(f32[2,512,128]{1,0,2:T(2,128)S(1)} %copy.366, f32[16,2,512]{2,1,0:T(2,128)S(1)} %get-tuple-element.264, f32[2,512,128]{1,0,2:T(2,128)S(1)} %copy.367, f32[16,2,512]{2,1,0:T(2,128)S(1)} %get-tuple-element.266), kind=kLoop, calls=%fused_computation.3.clone.1 | loop fusion | flops 16777216 | bytes 9568256 | tf_op jit(solution)/shard_map/convert.2
  633.5 20.3 %pad_maximum_fusion.3 = bf16[16,2,2,512,128]{3,2,1,4,0:T(2,128)(2,1)} fusion(bf16[16,2,1,512,128]{3,2,1,4,0:T(2,128)(2,1)S(1)} %get-tuple-element.267, bf16[16,2,1,512,128]{3,2,1,4,0:T(2,128)(2,1)S(1)} %get-tuple-element.268), kind=kLoop, calls=%fused_computation.1.clone.1 | loop fusion | flops 16777216 | bytes 16777216 | tf_op jit(solution)/shard_map/while/body/eval_jaxpr/stack | solution.py:116
  653.8 14.5 %convert_element_type.104 = bf16[16,2048,128]{1,2,0:T(8,128)(2,1)} reshape(bf16[16,2,2,512,128]{3,2,1,4,0:T(2,128)(2,1)} %pad_maximum_fusion.3) | data formatting | bytes 16777216 | tf_op jit(solution)/shard_map/while/body/eval_jaxpr/convert_element_type | solution.py:118
  668.3 11.4 %fusion.294 = f32[8,16,128,128]{3,2,1,0:T(8,128)} fusion(f32[8,16,128,128]{3,2,1,0:T(8,128)} %get-tuple-element.278, s32[]{:T(128)} %get-tuple-element.277, bf16[16,2048,128]{1,2,0:T(8,128)(2,1)} %convert_element_type.104, s32[128]{0:T(128)S(1)} %get-tuple-element.289, s32[2048]{0:T(1024)S(1)} %get-tuple-element.290, ...), kind=kOutput, calls=%fused_computation.10.clone.1 | convolution fusion | flops 1078198272 | bytes 9448448 | tf_op jit(solution)/shard_map/while/body/eval_jaxpr/bfc,ft->bct/dot_general | solution.py:130
  680.6 17.8 %add_convert_fusion.2 = (bf16[16,2,1,512,128]{3,2,1,4,0:T(2,128)(2,1)S(1)}, bf16[16,2,1,512,128]{3,2,1,4,0:T(2,128)(2,1)S(1)}) fusion(f32[2,512,128]{1,0,2:T(2,128)S(1)} %copy.366, f32[16,2,512]{2,1,0:T(2,128)S(1)} %get-tuple-element.264, f32[2,512,128]{1,0,2:T(2,128)S(1)} %copy.367, f32[16,2,512]{2,1,0:T(2,128)S(1)} %get-tuple-element.266), kind=kLoop, calls=%fused_computation.3.clone.1 | loop fusion | flops 16777216 | bytes 9568256 | tf_op jit(solution)/shard_map/convert.2
  698.5 20.3 %pad_maximum_fusion.3 = bf16[16,2,2,512,128]{3,2,1,4,0:T(2,128)(2,1)} fusion(bf16[16,2,1,512,128]{3,2,1,4,0:T(2,128)(2,1)S(1)} %get-tuple-element.267, bf16[16,2,1,512,128]{3,2,1,4,0:T(2,128)(2,1)S(1)} %get-tuple-element.268), kind=kLoop, calls=%fused_computation.1.clone.1 | loop fusion | flops 16777216 | bytes 16777216 | tf_op jit(solution)/shard_map/while/body/eval_jaxpr/stack | solution.py:116
  718.8 14.5 %convert_element_type.104 = bf16[16,2048,128]{1,2,0:T(8,128)(2,1)} reshape(bf16[16,2,2,512,128]{3,2,1,4,0:T(2,128)(2,1)} %pad_maximum_fusion.3) | data formatting | bytes 16777216 | tf_op jit(solution)/shard_map/while/body/eval_jaxpr/convert_element_type | solution.py:118
  733.3 11.4 %fusion.294 = f32[8,16,128,128]{3,2,1,0:T(8,128)} fusion(f32[8,16,128,128]{3,2,1,0:T(8,128)} %get-tuple-element.278, s32[]{:T(128)} %get-tuple-element.277, bf16[16,2048,128]{1,2,0:T(8,128)(2,1)} %convert_element_type.104, s32[128]{0:T(128)S(1)} %get-tuple-element.289, s32[2048]{0:T(1024)S(1)} %get-tuple-element.290, ...), kind=kOutput, calls=%fused_computation.10.clone.1 | convolution fusion | flops 1078198272 | bytes 9448448 | tf_op jit(solution)/shard_map/while/body/eval_jaxpr/bfc,ft->bct/dot_general | solution.py:130
  745.2 0.2 copy.366
  745.4 0.2 copy.367
  745.6 17.8 %add_convert_fusion.2 = (bf16[16,2,1,512,128]{3,2,1,4,0:T(2,128)(2,1)S(1)}, bf16[16,2,1,512,128]{3,2,1,4,0:T(2,128)(2,1)S(1)}) fusion(f32[2,512,128]{1,0,2:T(2,128)S(1)} %copy.366, f32[16,2,512]{2,1,0:T(2,128)S(1)} %get-tuple-element.264, f32[2,512,128]{1,0,2:T(2,128)S(1)} %copy.367, f32[16,2,512]{2,1,0:T(2,128)S(1)} %get-tuple-element.266), kind=kLoop, calls=%fused_computation.3.clone.1 | loop fusion | flops 16777216 | bytes 9568256 | tf_op jit(solution)/shard_map/convert.2
  763.5 20.3 %pad_maximum_fusion.3 = bf16[16,2,2,512,128]{3,2,1,4,0:T(2,128)(2,1)} fusion(bf16[16,2,1,512,128]{3,2,1,4,0:T(2,128)(2,1)S(1)} %get-tuple-element.267, bf16[16,2,1,512,128]{3,2,1,4,0:T(2,128)(2,1)S(1)} %get-tuple-element.268), kind=kLoop, calls=%fused_computation.1.clone.1 | loop fusion | flops 16777216 | bytes 16777216 | tf_op jit(solution)/shard_map/while/body/eval_jaxpr/stack | solution.py:116
  783.8 14.5 %convert_element_type.104 = bf16[16,2048,128]{1,2,0:T(8,128)(2,1)} reshape(bf16[16,2,2,512,128]{3,2,1,4,0:T(2,128)(2,1)} %pad_maximum_fusion.3) | data formatting | bytes 16777216 | tf_op jit(solution)/shard_map/while/body/eval_jaxpr/convert_element_type | solution.py:118
  798.3 11.4 %fusion.294 = f32[8,16,128,128]{3,2,1,0:T(8,128)} fusion(f32[8,16,128,128]{3,2,1,0:T(8,128)} %get-tuple-element.278, s32[]{:T(128)} %get-tuple-element.277, bf16[16,2048,128]{1,2,0:T(8,128)(2,1)} %convert_element_type.104, s32[128]{0:T(128)S(1)} %get-tuple-element.289, s32[2048]{0:T(1024)S(1)} %get-tuple-element.290, ...), kind=kOutput, calls=%fused_computation.10.clone.1 | convolution fusion | flops 1078198272 | bytes 9448448 | tf_op jit(solution)/shard_map/while/body/eval_jaxpr/bfc,ft->bct/dot_general | solution.py:130
  810.2 0.2 copy.366
  810.4 0.2 copy.367
  810.6 17.8 %add_convert_fusion.2 = (bf16[16,2,1,512,128]{3,2,1,4,0:T(2,128)(2,1)S(1)}, bf16[16,2,1,512,128]{3,2,1,4,0:T(2,128)(2,1)S(1)}) fusion(f32[2,512,128]{1,0,2:T(2,128)S(1)} %copy.366, f32[16,2,512]{2,1,0:T(2,128)S(1)} %get-tuple-element.264, f32[2,512,128]{1,0,2:T(2,128)S(1)} %copy.367, f32[16,2,512]{2,1,0:T(2,128)S(1)} %get-tuple-element.266), kind=kLoop, calls=%fused_computation.3.clone.1 | loop fusion | flops 16777216 | bytes 9568256 | tf_op jit(solution)/shard_map/convert.2
  828.5 20.3 %pad_maximum_fusion.3 = bf16[16,2,2,512,128]{3,2,1,4,0:T(2,128)(2,1)} fusion(bf16[16,2,1,512,128]{3,2,1,4,0:T(2,128)(2,1)S(1)} %get-tuple-element.267, bf16[16,2,1,512,128]{3,2,1,4,0:T(2,128)(2,1)S(1)} %get-tuple-element.268), kind=kLoop, calls=%fused_computation.1.clone.1 | loop fusion | flops 16777216 | bytes 16777216 | tf_op jit(solution)/shard_map/while/body/eval_jaxpr/stack | solution.py:116
  848.8 14.5 %convert_element_type.104 = bf16[16,2048,128]{1,2,0:T(8,128)(2,1)} reshape(bf16[16,2,2,512,128]{3,2,1,4,0:T(2,128)(2,1)} %pad_maximum_fusion.3) | data formatting | bytes 16777216 | tf_op jit(solution)/shard_map/while/body/eval_jaxpr/convert_element_type | solution.py:118
  863.3 11.4 %fusion.294 = f32[8,16,128,128]{3,2,1,0:T(8,128)} fusion(f32[8,16,128,128]{3,2,1,0:T(8,128)} %get-tuple-element.278, s32[]{:T(128)} %get-tuple-element.277, bf16[16,2048,128]{1,2,0:T(8,128)(2,1)} %convert_element_type.104, s32[128]{0:T(128)S(1)} %get-tuple-element.289, s32[2048]{0:T(1024)S(1)} %get-tuple-element.290, ...), kind=kOutput, calls=%fused_computation.10.clone.1 | convolution fusion | flops 1078198272 | bytes 9448448 | tf_op jit(solution)/shard_map/while/body/eval_jaxpr/bfc,ft->bct/dot_general | solution.py:130
  874.7 6.5 multiply_convert_fusion
  (76 shorter events, 5.8 us)
Async XLA Ops:
  6.5 143.3 %reduce-scatter.2.cloned.1.call-start = ((), (), s32[]{:S(2)}) async-start(), calls=%async_computation.1 | async-start | bytes 1572864 | tf_op jit(solution)/shard_map/reduce_scatter | solution.py:147
  8.5 14.4 %collective-permute-start = (f32[128,64]{0,1:T(8,128)S(1)}, f32[128,64]{0,1:T(8,128)S(1)}, u32[]{:S(2)}, u32[]{:S(2)}) collective-permute-start(f32[128,64]{0,1:T(8,128)S(1)} %slice.573), channel_id=1, source_target_pairs={{0,128},{1,129},{2,130},{3,131},{4,132},{5,133},{6,134},{7,135},{8... | collective-permute-start | bytes 98312 | tf_op jit(solution)/shard_map/ppermute | solution.py:20
  65.5 44.1 %copy-start = (s32[2]{0:T(128)S(1)}, s32[2]{0:T(128)}, u32[]{:S(2)}) copy-start(s32[2]{0:T(128)} %param.9) | copy-start | bytes 28
Sparse Core Ops, SparseCore 0:
  109.7 40.0 reduce-scatter.1
where the time goes:
time: 892 us; the launch traced here: 888 us
  other arithmetic  325 us (36%)
  blocking collectives  201 us (23%)
  local copies, waits for them, and re-layouts  162 us (18%)
  matrix products  137 us (15%)
  waiting for transfers between devices  39.6 us (4%)
  between operations  13.6 us (2%)
  starting transfers between devices  9.65 us (1%)
    all_gather x1, blocking collectives, per_device(): lax.all_gather(chosen, 'rcv', axis=1, tiled=True)  187 us
    another operation x8, other arithmetic, cross_block(): jnp.stack([cross_re, cross_im], axis=2)  163 us
    another operation x8, other arithmetic  143 us
    convert_element_type x8, local copies, waits for them, and re-layouts, cross_block(): return jnp.stack([cross_re, cross_im], axis=2).reshape(block_size, row_co...  116 us
    dot_general x8, matrix products, per_block(): jnp.einsum('bfc,ft->bct', cross, table, preferred_element_type=jnp.float32)  91.2 us
    dot_general x1, matrix products, spectrum_block(): lax.dot_general(dft_table, traces, (((1,), (1,)), ((), ())), precision=la...  44.1 us
    reduce_scatter x1, waiting for transfers between devices, per_device(): lax.psum_scatter(spectrum_block(jnp.arange(FREQ * lax.axis_size('sec'), d...  39.6 us
    slice x4, local copies, waits for them, and re-layouts, decimate(): frames[:, phase, shift_pos:shift_pos + samples]  33.6 us
  transfers between devices with their start and end apart: 2, of which 1 were waited for; matrix products, arithmetic and copies ran while one was open for 1% of the time, Pallas kernels for 0%

commit v1 on v0

v1 whole, which is shorter than its diff:
```python
import functools

import jax
import jax.numpy as jnp
import ml_dtypes
import numpy as np
from jax import lax
from jax.experimental import pallas as pl
from jax.experimental.pallas import tpu as pltpu
from jax.sharding import PartitionSpec as P

TD = 2048
HALF = 1024
TAPS = 64
CH = 128
NA = 16
NB = 8
SHAPE = (4, 4, 4, 2)
NN = (((1,), (0,)), ((), ()))
NT = (((1,), (1,)), ((), ()))
F32 = jnp.float32
BF16 = jnp.bfloat16


def bins(odd):
    col = np.arange(512)
    rank = col // 128 * 8 + col % 128 // 16
    return 64 * (col % 16) + 2 * rank + odd


def split_table(table):
    high = table.astype(ml_dtypes.bfloat16)
    low = (table - high.astype(np.float64)).astype(ml_dtypes.bfloat16)
    return np.stack([high, low])


def cot(num):
    return 1.0 / np.tan(np.pi * num / TD)


@functools.cache
def tables():
    even, odd = bins(0), bins(1)
    time = np.arange(HALF)[:, None]

    def wave(freq, times):
        ang = 2 * np.pi * (freq[None, :] * times % TD) / TD
        return np.cos(ang), -np.sin(ang)

    re, im = wave(even, time)
    nyquist = (-1.0) ** np.arange(HALF)
    im = im.copy()
    im[:, 0] = nyquist
    dft = np.concatenate([re, im], 1)
    fe, fo = even[:, None], odd[None, :]
    mix = np.zeros((HALF, HALF))
    norm = np.where(even == 0, 1.0 / HALF, 2.0 / HALF)[:, None]
    mix[:512, :512] = norm
    mix[:512, 512:] = -0.5 * (cot(fe + fo) + cot(fo - fe)) * norm
    mix[512:, :512] = -0.5 * (cot(fe + fo) + cot(fe - fo)) * norm
    mix[512, :512] = 1.0 / HALF
    mix[512, 512:] = (-0.5 * (cot(HALF + fo) + cot(fo - HALF)) / HALF)[0]
    tail = np.zeros((128, TD))
    rows = np.arange(16)[:, None]
    tail[:16] = np.concatenate(wave(even, rows) + tuple(-w for w in wave(odd, rows)), 1)
    both = np.concatenate([even, odd])[None, :]
    shift = 2 * np.pi * (both * np.arange(NB)[:, None] % TD) / TD
    coarse = 2 * np.pi * (both * (NB * np.arange(NA)[:, None] - 64) % TD) / TD
    place = np.zeros((TAPS, 640), np.float32)
    place[np.arange(TAPS), 128 - np.arange(TAPS)] = 1.0
    return dict(
        dft=split_table(dft),
        mix=split_table(mix),
        tail=split_table(tail),
        shift=np.stack([np.cos(shift), np.sin(shift)]).astype(np.float32),
        coarse=(np.stack([np.cos(coarse), np.sin(coarse)]) / 32.0).astype(np.float32),
        place=place,
    )


def split(values):
    high = values.astype(BF16)
    return high, (values - high.astype(F32)).astype(BF16)


def dot3(left, right, dims=NN):
    (lh, ll), (rh, rl) = left, right
    dot = functools.partial(lax.dot_general, dimension_numbers=dims, preferred_element_type=F32)
    return dot(lh, rh) + (dot(ll, rh) + dot(lh, rl))


def prepare_kernel(
    place_idx, strain, offset, fir, place, dft, e32, e16, tail_out, own_msg, far_msg, ext, dec
):
    sec = place_idx[0]
    width = ext.shape[1]
    ext[:, :128] = jnp.zeros((CH, 128), F32)
    ext[:, width - 128 :] = jnp.zeros((CH, 128), F32)
    ext[:, 128 : width - 128] = strain[...]
    taps = jnp.broadcast_to(fir[...], (8, TAPS))
    row = lax.dot_general(
        taps, place[...], NN, precision=lax.Precision.HIGHEST, preferred_element_type=F32
    )
    band = pltpu.roll(jnp.broadcast_to(row[:1], (128, 640)), 0, 1, stride=4, stride_axis=0)
    band = split(band)
    off = offset[...]
    raw = ext[...]
    shifted = raw
    for step in range(1, 4):
        shifted = jnp.where(off == step, pltpu.roll(raw, width - step, 1), shifted)
    high, low = split(shifted)
    for block in range(8):
        at = slice(512 * block, 512 * block + 640)
        dec[:, 128 * block : 128 * block + 128] = dot3((high[:, at], low[:, at]), band, NT)
    at = slice(4096, 4352)
    seam = dot3((high[:, at], low[:, at]), (band[0][:, :256], band[1][:, :256]), NT)
    seam = jnp.where(sec == 0, seam, 0.0)
    tail_out[...] = seam
    even = dot3(split(dec[...]), (dft[0], dft[1]))
    e32[...] = even
    e16[...] = even.astype(BF16)
    for slot, msg in ((sec, own_msg), (1 - sec, far_msg)):
        src = place_idx[1 + slot]
        values = e32[pl.ds(src, 1), :]
        for part in range(8):
            msg[part : part + 1, :] = values[:, 128 * part : 128 * part + 128]
        msg[8:9, :] = tail_out[pl.ds(src, 1), :]
        msg[9:16, :] = jnp.zeros((7, 128), F32)
    far_msg[16:32, :] = seam.T[:16]


def whole_window(own, far, seam, sign, mix, tail):
    even = own + far
    odd = dot3(split((own - far) * sign), mix)
    added = dot3(split(seam), tail)
    even = even + added[:, :HALF]
    odd = odd + added[:, HALF:]
    column = lax.broadcasted_iota(jnp.int32, even.shape, 1)
    even = jnp.where(column == 512, 0.0, even)
    spectrum = jnp.concatenate([even, odd], 1)
    power = jnp.zeros((own.shape[0], 128), F32)
    for part in range(16):
        piece = spectrum[:, 128 * part : 128 * part + 128]
        power = power + piece * piece
    for step in (16, 32, 64):
        power = power + pltpu.roll(power, step, 1)
    factor = 1.0 / jnp.sqrt(power * (1.0 / 128.0) + 1e-06)
    return spectrum * jnp.concatenate([factor] * 16, 1)


def source_kernel(place_idx, own, far, mix, tail, out):
    sec = place_idx[0]
    sign = jnp.where(sec == 0, 1.0, -1.0).astype(F32)

    def line(ref):
        return jnp.concatenate([ref[part : part + 1, :] for part in range(8)], 1)

    def rows(values):
        return jnp.broadcast_to(values, (8, values.shape[1]))

    seam = jnp.where(sec == 0, own[8:9, :], far[8:9, :])
    white = whole_window(
        rows(line(own)), rows(line(far)), rows(seam), sign, (mix[0], mix[1]), (tail[0], tail[1])
    )
    parts = [white[:1, 128 * part : 128 * part + 128] for part in range(16)]
    out[...] = jnp.concatenate(parts, 0).astype(BF16)


def receiver_kernel(place_idx, own, far, own_tail, far_tail, mix, tail, coarse, out):
    sec = place_idx[0]
    sign = jnp.where(sec == 0, 1.0, -1.0).astype(F32)
    seam = jnp.where(sec == 0, own_tail[...], far_tail[...])
    white = whole_window(
        own[...], far[...].astype(F32), seam, sign, (mix[0], mix[1]), (tail[0], tail[1])
    )

    def lag(a, carry):
        for half in (0, 1):
            at = HALF * half
            re = white[:, at : at + 512]
            im = white[:, at + 512 : at + HALF]
            cos = coarse[0, pl.ds(a, 1), 512 * half : 512 * half + 512]
            sin = coarse[1, pl.ds(a, 1), 512 * half : 512 * half + 512]
            out[a, :, at : at + 512] = (re * cos - im * sin).astype(BF16)
            out[a, :, at + 512 : at + HALF] = (re * sin + im * cos).astype(BF16)
        return carry

    lax.fori_loop(0, NA, lag, 0)


def correlate_kernel(place_idx, chosen, turned, shift, out, left, sums):
    step = pl.program_id(0)

    @pl.when(step == 0)
    def _():
        def pair(two, carry):
            parts = [chosen[2 * two + k].astype(F32) for k in range(2)]
            at = pl.ds(pl.multiple_of(16 * two, 16), 16)
            for half in (0, 1):
                for part in range(4):
                    row = 8 * half + part
                    lane = 512 * half + 128 * part
                    cos = shift[0, :, lane : lane + 128]
                    sin = shift[1, :, lane : lane + 128]
                    re = [jnp.broadcast_to(p[row : row + 1], (NB, 128)) for p in parts]
                    im = [jnp.broadcast_to(p[row + 4 : row + 5], (NB, 128)) for p in parts]
                    col = 1024 * half + 128 * part
                    left[at, col : col + 128] = jnp.concatenate(
                        [re[k] * cos + im[k] * sin for k in range(2)], 0
                    ).astype(BF16)
                    left[at, col + 512 : col + 640] = jnp.concatenate(
                        [im[k] * cos - re[k] * sin for k in range(2)], 0
                    ).astype(BF16)
            return carry

        lax.fori_loop(0, 64, pair, 0)

    width = turned.shape[0]
    total = lax.dot_general(
        left[...], turned[...].reshape(width * CH, TD), NT, preferred_element_type=F32
    )
    for k in range(width):
        sums[step * width + k] = total[:, CH * k : CH * k + CH]

    @pl.when(step == pl.num_programs(0) - 1)
    def _():
        y, z, x, core = (place_idx[k] for k in range(4))

        def finish(rel, carry):
            dc, dx, dy, dz = rel // 64, rel // 16 % 4, rel // 4 % 4, rel % 4
            block = (
                (lax.rem(y - dy + 4, 4) * 4 + lax.rem(z - dz + 4, 4)) * 4 + lax.rem(x - dx + 4, 4)
            ) * 2 + lax.rem(core + dc, 2)
            at = pl.ds(pl.multiple_of(rel * NB, NB), NB)
            tile = sums[:, at, :].reshape(NA * NB, CH)
            out[block] = tile.T.astype(BF16)
            return carry

        lax.fori_loop(0, 128, finish, 0, unroll=4)


def vmem(count):
    return [pl.BlockSpec(memory_space=pltpu.VMEM)] * count


SMEM = pl.BlockSpec(memory_space=pltpu.SMEM)
LIMIT = pltpu.CompilerParams(vmem_limit_bytes=56 * 2**20)


def prepare(place_idx, strain, offset, fir, tab):
    width = strain.shape[1] + 256
    shapes = [((CH, HALF), F32), ((CH, HALF), BF16), ((CH, 128), F32), ((16, 128), F32), ((32, 128), F32)]
    return pl.pallas_call(
        prepare_kernel,
        out_shape=[jax.ShapeDtypeStruct(*s) for s in shapes],
        in_specs=[SMEM] + vmem(5),
        out_specs=vmem(5),
        scratch_shapes=[pltpu.VMEM((CH, width), F32), pltpu.VMEM((CH, HALF), F32)],
        compiler_params=LIMIT,
        name="prepare",
    )(place_idx, strain, offset, fir, tab["place"], tab["dft"])


def finish_sources(place_idx, own, far, tab):
    return pl.pallas_call(
        source_kernel,
        out_shape=jax.ShapeDtypeStruct((16, 128), BF16),
        in_specs=[SMEM] + vmem(4),
        out_specs=vmem(1)[0],
        compiler_params=LIMIT,
        name="finish_sources",
    )(place_idx, own, far, tab["mix"], tab["tail"])


def turn_receivers(place_idx, own, far, own_tail, far_tail, tab):
    rows = 32

    def whole(*shape):
        return pl.BlockSpec(shape, lambda c: (0,) * len(shape))

    def part(*shape):
        return pl.BlockSpec(shape, lambda c: (c, 0))

    return pl.pallas_call(
        receiver_kernel,
        grid=(CH // rows,),
        out_shape=jax.ShapeDtypeStruct((NA, CH, TD), BF16),
        in_specs=[
            SMEM,
            part(rows, HALF),
            part(rows, HALF),
            part(rows, 128),
            part(rows, 128),
            whole(2, HALF, HALF),
            whole(2, 128, TD),
            whole(2, NA, HALF),
        ],
        out_specs=pl.BlockSpec((NA, rows, TD), lambda c: (0, c, 0)),
        compiler_params=LIMIT,
        cost_estimate=pl.CostEstimate(flops=3 * 2 * 128 * 1024 * 1024, bytes_accessed=16 * 2**20, transcendentals=0),
        name="turn_receivers",
    )(place_idx, own, far, own_tail, far_tail, tab["mix"], tab["tail"], tab["coarse"])


def correlate(where, chosen, turned, tab):
    width = 4
    return pl.pallas_call(
        correlate_kernel,
        grid=(NA // width,),
        out_shape=jax.ShapeDtypeStruct((128, CH, 128), BF16),
        in_specs=[
            SMEM,
            pl.BlockSpec((128, 16, 128), lambda n: (0, 0, 0)),
            pl.BlockSpec((width, CH, TD), lambda n: (n, 0, 0)),
            pl.BlockSpec((2, NB, HALF), lambda n: (0, 0, 0)),
        ],
        out_specs=pl.BlockSpec((128, CH, 128), lambda n: (0, 0, 0)),
        scratch_shapes=[pltpu.VMEM((128 * NB, TD), BF16), pltpu.VMEM((NA, 128 * NB, CH), F32)],
        compiler_params=LIMIT,
        cost_estimate=pl.CostEstimate(flops=2 * 2**32, bytes_accessed=13 * 2**20, transcendentals=0),
        name="correlate",
    )(where, chosen, turned, tab["shift"])


def coordinates(index):
    y, z, x, core = SHAPE
    return [index // (z * x * core), index // (x * core) % z, index // core % x, index % core]


def around(values, dim, by):
    def target(index):
        at = coordinates(index)
        at[dim] = (at[dim] + by) % SHAPE[dim]
        return ((at[0] * SHAPE[1] + at[1]) * SHAPE[2] + at[2]) * SHAPE[3] + at[3]

    return lax.ppermute(values, "rcv", [(i, target(i)) for i in range(int(np.prod(SHAPE)))])


def gather(values):
    values = values[None]
    for dim in (1, 0, 2, 3):
        values = jnp.concatenate(
            [values] + [around(values, dim, by) for by in range(1, SHAPE[dim])], 0
        )
    return values


def per_device(strain, offset, fir_taps, source_channel):
    tab = tables()
    sec = lax.axis_index("sec").astype(jnp.int32)
    rcv = lax.axis_index("rcv").astype(jnp.int32)
    place_idx = jnp.concatenate([sec[None], source_channel.astype(jnp.int32)])
    where = jnp.stack(coordinates(rcv))
    e32, e16, own_tail, own_msg, far_msg = prepare(
        place_idx, strain, offset[:, None], fir_taps[None, :], tab
    )
    swap = [(0, 1), (1, 0)]
    got_msg = lax.ppermute(far_msg, "sec", swap)
    got16 = lax.ppermute(e16, "sec", swap)
    chosen = gather(finish_sources(place_idx, own_msg, got_msg[:16], tab))
    far_tail = jnp.pad(got_msg[16:].T, ((0, 0), (0, 112)))
    turned = turn_receivers(place_idx, e32, got16, own_tail, far_tail, tab)
    return correlate(where, chosen, turned, tab)[None]


def solution(mesh):
    in_specs = (P("rcv", "sec"), P("rcv"), P(), P("rcv"))
    out_specs = P("sec", None, "rcv", None)
    return jax.shard_map(
        per_device, mesh=mesh, in_specs=in_specs, out_specs=out_specs, check_vma=False
    )
```

time: 892 us -> 96.2 us (0.11)
  other arithmetic: 325 us -> 2.59 us
  blocking collectives: 201 us -> 0 us
  local copies, waits for them, and re-layouts: 162 us -> 6.12 us
  matrix products: 137 us -> 0 us
  Pallas kernels: 0 us -> 43.5 us
  waiting for transfers between devices: 39.6 us -> 11.5 us
  starting transfers between devices: 9.65 us -> 32.2 us
  between operations: 13.6 us -> 0.09 us
    another operation x16 -> x1, other arithmetic: 305 us -> 0.67 us  [per_device(): where = jnp.stack(coordinates(rcv))]
    all_gather x2 -> x0, blocking collectives: 201 us -> none  [the longest x1 187 us: per_device(): lax.all_gather(chosen, 'rcv', axis=1, tiled=True)]
    dot_general x11 -> x0, matrix products: 137 us -> none  [the longest x8 91.2 us: per_block(): jnp.einsum('bfc,ft->bct', cross, table, preferred_element_type=jnp.float32)]
    convert_element_type x16 -> x0, local copies, waits for them, and re-layouts: 117 us -> none  [the longest x8 116 us: cross_block(): return jnp.stack([cross_re, cross_im], axis=2).reshape(block_size, row_co...]
    pallas_call x0 -> x4, Pallas kernels: none -> 43.5 us  [the longest x1 18.7 us: correlate(): pl.pallas_call(correlate_kernel, grid=(NA // width,), out_shape=jax.Shape...]
    reduce_scatter x1 -> x0, waiting for transfers between devices: 39.6 us -> none  [per_device(): lax.psum_scatter(spectrum_block(jnp.arange(FREQ * lax.axis_size('sec'), d...]
    slice x13 -> x1, local copies, waits for them, and re-layouts: 34.4 us -> 0.68 us  [per_device(): chosen = gather(finish_sources(place_idx, own_msg, got_msg[:16], tab))]
    ppermute x1 -> x12, starting transfers between devices: 9.64 us -> 32.2 us  [the longest x10 19.6 us: around(): lax.ppermute(values, 'rcv', [(i, target(i)) for i in range(int(np.prod(SH...]
  transfers between devices with their start and end apart: 2 -> 12, of which waited for: 1 -> 5; matrix products, arithmetic and copies ran while one was open for 1% -> 2% of each run, Pallas kernels for 0% -> 14%
where the time goes in v1:
time: 96.2 us; the launch traced here: 95.9 us
  Pallas kernels  43.5 us (45%)
  starting transfers between devices  32.2 us (33%)
  waiting for transfers between devices  11.5 us (12%)
  local copies, waits for them, and re-layouts  6.12 us (6%)
  other arithmetic  2.59 us (3%)
    ppermute x10, starting transfers between devices, around(): lax.ppermute(values, 'rcv', [(i, target(i)) for i in range(int(np.prod(SH...  19.6 us
    pallas_call x1, Pallas kernels, correlate(): pl.pallas_call(correlate_kernel, grid=(NA // width,), out_shape=jax.Shape...  18.7 us
    pallas_call x1, Pallas kernels, turn_receivers(): pl.pallas_call(receiver_kernel, grid=(CH // rows,), out_shape=jax.ShapeDt...  13.3 us
    ppermute x10, waiting for transfers between devices, around(): lax.ppermute(values, 'rcv', [(i, target(i)) for i in range(int(np.prod(SH...  9.72 us
    ppermute x1, starting transfers between devices, per_device(): got_msg = lax.ppermute(far_msg, 'sec', swap)  7.83 us
    pallas_call x1, Pallas kernels, prepare(): pl.pallas_call(prepare_kernel, out_shape=[jax.ShapeDtypeStruct(*s) for s...  7.01 us
    ppermute x1, starting transfers between devices, per_device(): got16 = lax.ppermute(e16, 'sec', swap)  4.7 us
    pallas_call x1, Pallas kernels, finish_sources(): pl.pallas_call(source_kernel, out_shape=jax.ShapeDtypeStruct((16, 128), B...  4.48 us
  transfers between devices with their start and end apart: 12, of which 5 were waited for; matrix products, arithmetic and copies ran while one was open for 2% of the time, Pallas kernels for 14%

profile of v1, /device:TPU:1, one launch (start us, length us, event | category | flops | bytes accessed | tf_op | source)
XLA Modules:
  0.0 95.9 jit_solution(2928365532758501518)
XLA Ops:
  0.0 1.4 %copy.11.offset = s32[128,1]{1,0:T(8,128)} copy(s32[128,1]{0,1:T(1,128)} %bitcast.18) | data formatting | bytes 1024 | tf_op jit(solution)/shard_map/broadcast_in_dim | solution.py:355
  1.4 1.2 %pad_add_fusion.1.place_idx = s32[3]{0:T(128)} fusion(s32[2]{0:T(128)} %param.13, s32[1]{0:T(128)} %bitcast.4), kind=kLoop, calls=%fused_computation.31 | loop fusion | flops 3 | bytes 24 | tf_op jit(solution)/shard_map/concatenate | solution.py:352
  2.6 7.0 %prepare.1 = (f32[128,1024]{1,0:T(8,128)}, bf16[128,1024]{1,0:T(8,128)(2,1)}, f32[128,128]{1,0:T(8,128)}, f32[16,128]{1,0:T(8,128)}, f32[32,128]{1,0:T(8,128)}) custom-call(s32[3]{0:T(128)} %pad_add_fusion.1.place_idx, f32[128,4096]{1,0:T(8,128)} %strain.1, s32[128,1]{1,0:T(8,128)} %copy.11.offset, f32[1,64]{1,0:T(1,128)} %bitcast.19, ...), custom_call_target="tpu_custom_call" | custom-call | tf_op jit(solution)/shard_map/prepare/pallas_call | solution.py:253
  9.6 0.0 copy-start.2
  9.6 0.9 copy.12
  10.5 7.8 %collective-permute-start = (f32[32,128]{0,1:T(8,128)S(1)}, f32[32,128]{0,1:T(8,128)S(1)}, u32[]{:S(2)}, u32[]{:S(2)}) collective-permute-start(f32[32,128]{0,1:T(8,128)S(1)} %copy.12), channel_id=1, source_target_pairs={{0,128},{128,0},{1,129},{129,1},{2,130},{130,2},{3,131},{131,3},{4... | collective-permute-start | bytes 49160 | tf_op jit(solution)/shard_map/ppermute | solution.py:358
  18.3 1.8 %collective-permute-done = f32[32,128]{0,1:T(8,128)S(1)} collective-permute-done((f32[32,128]{0,1:T(8,128)S(1)}, f32[32,128]{0,1:T(8,128)S(1)}, u32[]{:S(2)}, u32[]{:S(2)}) %collective-permute-start) | collective-permute-done | bytes 16416 | tf_op jit(solution)/shard_map/ppermute | solution.py:358
  20.1 0.1 slice_bitcast_fusion
  20.1 0.7 copy.13.far
  20.8 4.5 %finish_sources.1 = bf16[16,128]{1,0:T(8,128)(2,1)} custom-call(s32[3]{0:T(128)} %pad_add_fusion.1.place_idx, f32[16,128]{1,0:T(8,128)} %get-tuple-element.10.own, f32[16,128]{1,0:T(8,128)} %copy.13.far, bf16[2,1024,1024]{2,1,0:T(8,128)(2,1)} %constant.85.clone.mix, bf16[2,128,2048]{2,1,0:T(8,128)(2,1)} %constant.86.clone.tail), custom_call_target="tpu_custom_call" | custom-call | tf_op jit(solution)/shard_map/finish_sources/pallas_call | solution.py:265
  25.3 2.7 %collective-permute-start.3 = (bf16[1,16,128]{2,1,0:T(8,128)(2,1)}, bf16[1,16,128]{2,1,0:T(8,128)(2,1)S(1)}, u32[]{:S(2)}, u32[]{:S(2)}) collective-permute-start(bf16[1,16,128]{2,1,0:T(8,128)(2,1)} %bitcast.14), channel_id=1, source_target_pairs={{0,24},{1,25},{2,26},{3,27},{4,28},{5,29},{6,30},{7,31},{8,0},{9,1... | collective-permute-start | bytes 12296 | tf_op jit(solution)/shard_map/ppermute | solution.py:336
  28.0 0.0 collective-permute-start.2
  28.0 0.3 collective-permute-start.1
  28.3 0.7 constant_dynamic-update-slice_fusion.16
  29.0 0.0 collective-permute-done.3
  29.0 2.6 %collective-permute-done.2 = bf16[1,16,128]{2,1,0:T(8,128)(2,1)S(1)} collective-permute-done((bf16[1,16,128]{2,1,0:T(8,128)(2,1)}, bf16[1,16,128]{2,1,0:T(8,128)(2,1)S(1)}, u32[]{:S(2)}, u32[]{:S(2)}) %collective-permute-start.2) | collective-permute-done | bytes 4128 | tf_op jit(solution)/shard_map/ppermute | solution.py:336
  31.6 0.9 collective-permute-done.1
  32.5 0.7 pad_maximum_fusion
  33.2 2.7 %collective-permute-start.6 = (bf16[4,16,128]{2,1,0:T(8,128)(2,1)S(1)}, bf16[4,16,128]{2,1,0:T(8,128)(2,1)S(1)}, u32[]{:S(2)}, u32[]{:S(2)}) collective-permute-start(bf16[4,16,128]{2,1,0:T(8,128)(2,1)S(1)} %pad_maximum_fusion), channel_id=1, source_target_pairs={{0,96},{1,97},{2,98},{3,99},{4,100},{5,101},{6,102},{7,103},{8,104... | collective-permute-start | bytes 49160 | tf_op jit(solution)/shard_map/ppermute | solution.py:336
  35.9 0.4 collective-permute-start.5
  36.3 0.7 collective-permute-start.4
  37.0 3.2 %collective-permute-done.4 = bf16[4,16,128]{2,1,0:T(8,128)(2,1)S(1)} collective-permute-done((bf16[4,16,128]{2,1,0:T(8,128)(2,1)S(1)}, bf16[4,16,128]{2,1,0:T(8,128)(2,1)S(1)}, u32[]{:S(2)}, u32[]{:S(2)}) %collective-permute-start.4) | collective-permute-done | bytes 16416 | tf_op jit(solution)/shard_map/ppermute | solution.py:336
  40.2 0.0 collective-permute-done.5
  40.2 0.0 collective-permute-done.6
  40.3 1.3 %collective-permute-start.7 = (bf16[16,16,128]{2,1,0:T(8,128)(2,1)S(1)}, bf16[16,16,128]{2,1,0:T(8,128)(2,1)S(1)}, u32[]{:S(2)}, u32[]{:S(2)}) collective-permute-start(bf16[16,16,128]{2,1,0:T(8,128)(2,1)S(1)} %get-tuple-element.25), channel_id=1, source_target_pairs={{0,2},{1,3},{2,4},{3,5},{4,6},{5,7},{6,0},{7,1},{8,10},{9,11},{10,... | collective-permute-start | bytes 196616 | tf_op jit(solution)/shard_map/ppermute | solution.py:336
  41.5 0.0 copy-done.2
  41.6 4.7 %collective-permute-start.11 = (bf16[128,1024]{1,0:T(8,128)(2,1)S(1)}, bf16[128,1024]{1,0:T(8,128)(2,1)S(1)}, u32[]{:S(2)}, u32[]{:S(2)}) collective-permute-start(bf16[128,1024]{1,0:T(8,128)(2,1)S(1)} %copy-done.2), channel_id=1, source_target_pairs={{0,128},{128,0},{1,129},{129,1},{2,130},{130,2},{3,131},{131,3},{4... | collective-permute-start | bytes 786440 | tf_op jit(solution)/shard_map/ppermute | solution.py:359
  46.3 1.5 %collective-permute-start.9 = (bf16[16,16,128]{2,1,0:T(8,128)(2,1)S(1)}, bf16[16,16,128]{2,1,0:T(8,128)(2,1)S(1)}, u32[]{:S(2)}, u32[]{:S(2)}) collective-permute-start(bf16[16,16,128]{2,1,0:T(8,128)(2,1)S(1)} %get-tuple-element.25), channel_id=1, source_target_pairs={{0,6},{1,7},{2,0},{3,1},{4,2},{5,3},{6,4},{7,5},{8,14},{9,15},{10,... | collective-permute-start | bytes 196616 | tf_op jit(solution)/shard_map/ppermute | solution.py:336
  47.7 1.5 %collective-permute-start.8 = (bf16[16,16,128]{2,1,0:T(8,128)(2,1)S(1)}, bf16[16,16,128]{2,1,0:T(8,128)(2,1)S(1)}, u32[]{:S(2)}, u32[]{:S(2)}) collective-permute-start(bf16[16,16,128]{2,1,0:T(8,128)(2,1)S(1)} %get-tuple-element.25), channel_id=1, source_target_pairs={{0,4},{1,5},{2,6},{3,7},{4,0},{5,1},{6,2},{7,3},{8,12},{9,13},{10,... | collective-permute-start | bytes 196616 | tf_op jit(solution)/shard_map/ppermute | solution.py:336
  49.3 0.0 collective-permute-done.7
  49.3 3.0 %collective-permute-done.8 = bf16[16,16,128]{2,1,0:T(8,128)(2,1)S(1)} collective-permute-done((bf16[16,16,128]{2,1,0:T(8,128)(2,1)S(1)}, bf16[16,16,128]{2,1,0:T(8,128)(2,1)S(1)}, u32[]{:S(2)}, u32[]{:S(2)}) %collective-permute-start.8) | collective-permute-done | bytes 65568 | tf_op jit(solution)/shard_map/ppermute | solution.py:336
  52.4 0.0 collective-permute-done.9
  52.4 8.6 %collective-permute-start.10 = (bf16[64,16,128]{2,1,0:T(8,128)(2,1)S(1)}, bf16[64,16,128]{2,1,0:T(8,128)(2,1)S(1)}, u32[]{:S(2)}, u32[]{:S(2)}) collective-permute-start(bf16[64,16,128]{2,1,0:T(8,128)(2,1)S(1)} %get-tuple-element.17), channel_id=1, source_target_pairs={{0,1},{1,0},{2,3},{3,2},{4,5},{5,4},{6,7},{7,6},{8,9},{9,8},{10,11... | collective-permute-start | bytes 786440 | tf_op jit(solution)/shard_map/ppermute | solution.py:336
  61.0 0.7 pad_add_fusion.place_idx
  61.6 0.6 pad.4.far_tail
  62.3 0.0 collective-permute-done.11.far
  62.3 0.0 copy-start
  62.3 0.7 copy-done
  63.0 13.3 %turn_receivers.1.turned = bf16[16,128,2048]{2,1,0:T(8,128)(2,1)} custom-call(s32[3]{0:T(128)} %pad_add_fusion.1.place_idx, f32[128,1024]{1,0:T(8,128)} %get-tuple-element.12.own, bf16[128,1024]{1,0:T(8,128)(2,1)} %copy-done, f32[128,128]{1,0:T(8,128)} %get-tuple-element.14.own_tail, f32[128,128]{1,0:T(8,128)} %pad.4.far_tail, ...), custom_call_target="tpu_custom_call" | custom-call | flops 805306368 | bytes 16777216 | tf_op jit(solution)/shard_map/turn_receivers/pallas_call | solution.py:284
  76.3 0.0 collective-permute-done.10
  76.3 0.0 copy-start.1
  76.3 0.8 copy-done.1
  77.2 18.7 %correlate.1 = bf16[128,128,128]{2,1,0:T(8,128)(2,1)} custom-call(s32[4]{0:T(128)} %pad_add_fusion.place_idx, bf16[128,16,128]{2,1,0:T(8,128)(2,1)} %copy-done.1, bf16[16,128,2048]{2,1,0:T(8,128)(2,1)} %turn_receivers.1.turned, f32[2,8,1024]{2,1,0:T(8,128)} %constant.88.clone.shift), custom_call_target="tpu_custom_call" | custom-call | flops 8589934592 | bytes 13631488 | tf_op jit(solution)/shard_map/correlate/pallas_call | solution.py:307
  (10 shorter events, 0.2 us)
Async XLA Ops:
  9.6 31.9 %copy-start.2 = (bf16[128,1024]{1,0:T(8,128)(2,1)S(1)}, bf16[128,1024]{1,0:T(8,128)(2,1)}, u32[]{:S(2)}) copy-start(bf16[128,1024]{1,0:T(8,128)(2,1)} %get-tuple-element.13) | copy-start | bytes 786436
  10.5 9.6 %collective-permute-start = (f32[32,128]{0,1:T(8,128)S(1)}, f32[32,128]{0,1:T(8,128)S(1)}, u32[]{:S(2)}, u32[]{:S(2)}) collective-permute-start(f32[32,128]{0,1:T(8,128)S(1)} %copy.12), channel_id=1, source_target_pairs={{0,128},{128,0},{1,129},{129,1},{2,130},{130,2},{3,131},{131,3},{4... | collective-permute-start | bytes 49160 | tf_op jit(solution)/shard_map/ppermute | solution.py:358
  25.3 3.7 %collective-permute-start.3 = (bf16[1,16,128]{2,1,0:T(8,128)(2,1)}, bf16[1,16,128]{2,1,0:T(8,128)(2,1)S(1)}, u32[]{:S(2)}, u32[]{:S(2)}) collective-permute-start(bf16[1,16,128]{2,1,0:T(8,128)(2,1)} %bitcast.14), channel_id=1, source_target_pairs={{0,24},{1,25},{2,26},{3,27},{4,28},{5,29},{6,30},{7,31},{8,0},{9,1... | collective-permute-start | bytes 12296 | tf_op jit(solution)/shard_map/ppermute | solution.py:336
  28.0 3.6 %collective-permute-start.2 = (bf16[1,16,128]{2,1,0:T(8,128)(2,1)}, bf16[1,16,128]{2,1,0:T(8,128)(2,1)S(1)}, u32[]{:S(2)}, u32[]{:S(2)}) collective-permute-start(bf16[1,16,128]{2,1,0:T(8,128)(2,1)} %bitcast.15), channel_id=1, source_target_pairs={{0,16},{1,17},{2,18},{3,19},{4,20},{5,21},{6,22},{7,23},{8,24},{9,... | collective-permute-start | bytes 12296 | tf_op jit(solution)/shard_map/ppermute | solution.py:336
  28.0 4.5 %collective-permute-start.1 = (bf16[1,16,128]{2,1,0:T(8,128)(2,1)}, bf16[1,16,128]{2,1,0:T(8,128)(2,1)S(1)}, u32[]{:S(2)}, u32[]{:S(2)}) collective-permute-start(bf16[1,16,128]{2,1,0:T(8,128)(2,1)} %bitcast.16), channel_id=1, source_target_pairs={{0,8},{1,9},{2,10},{3,11},{4,12},{5,13},{6,14},{7,15},{8,16},{9,17... | collective-permute-start | bytes 12296 | tf_op jit(solution)/shard_map/ppermute | solution.py:336
  33.2 7.1 %collective-permute-start.6 = (bf16[4,16,128]{2,1,0:T(8,128)(2,1)S(1)}, bf16[4,16,128]{2,1,0:T(8,128)(2,1)S(1)}, u32[]{:S(2)}, u32[]{:S(2)}) collective-permute-start(bf16[4,16,128]{2,1,0:T(8,128)(2,1)S(1)} %pad_maximum_fusion), channel_id=1, source_target_pairs={{0,96},{1,97},{2,98},{3,99},{4,100},{5,101},{6,102},{7,103},{8,104... | collective-permute-start | bytes 49160 | tf_op jit(solution)/shard_map/ppermute | solution.py:336
  35.9 4.3 %collective-permute-start.5 = (bf16[4,16,128]{2,1,0:T(8,128)(2,1)S(1)}, bf16[4,16,128]{2,1,0:T(8,128)(2,1)S(1)}, u32[]{:S(2)}, u32[]{:S(2)}) collective-permute-start(bf16[4,16,128]{2,1,0:T(8,128)(2,1)S(1)} %pad_maximum_fusion), channel_id=1, source_target_pairs={{0,64},{1,65},{2,66},{3,67},{4,68},{5,69},{6,70},{7,71},{8,72},{9,... | collective-permute-start | bytes 49160 | tf_op jit(solution)/shard_map/ppermute | solution.py:336
  36.3 3.9 %collective-permute-start.4 = (bf16[4,16,128]{2,1,0:T(8,128)(2,1)S(1)}, bf16[4,16,128]{2,1,0:T(8,128)(2,1)S(1)}, u32[]{:S(2)}, u32[]{:S(2)}) collective-permute-start(bf16[4,16,128]{2,1,0:T(8,128)(2,1)S(1)} %pad_maximum_fusion), channel_id=1, source_target_pairs={{0,32},{1,33},{2,34},{3,35},{4,36},{5,37},{6,38},{7,39},{8,40},{9,... | collective-permute-start | bytes 49160 | tf_op jit(solution)/shard_map/ppermute | solution.py:336
  40.3 9.0 %collective-permute-start.7 = (bf16[16,16,128]{2,1,0:T(8,128)(2,1)S(1)}, bf16[16,16,128]{2,1,0:T(8,128)(2,1)S(1)}, u32[]{:S(2)}, u32[]{:S(2)}) collective-permute-start(bf16[16,16,128]{2,1,0:T(8,128)(2,1)S(1)} %get-tuple-element.25), channel_id=1, source_target_pairs={{0,2},{1,3},{2,4},{3,5},{4,6},{5,7},{6,0},{7,1},{8,10},{9,11},{10,... | collective-permute-start | bytes 196616 | tf_op jit(solution)/shard_map/ppermute | solution.py:336
  41.6 20.7 %collective-permute-start.11 = (bf16[128,1024]{1,0:T(8,128)(2,1)S(1)}, bf16[128,1024]{1,0:T(8,128)(2,1)S(1)}, u32[]{:S(2)}, u32[]{:S(2)}) collective-permute-start(bf16[128,1024]{1,0:T(8,128)(2,1)S(1)} %copy-done.2), channel_id=1, source_target_pairs={{0,128},{128,0},{1,129},{129,1},{2,130},{130,2},{3,131},{131,3},{4... | collective-permute-start | bytes 786440 | tf_op jit(solution)/shard_map/ppermute | solution.py:359
  46.3 6.1 %collective-permute-start.9 = (bf16[16,16,128]{2,1,0:T(8,128)(2,1)S(1)}, bf16[16,16,128]{2,1,0:T(8,128)(2,1)S(1)}, u32[]{:S(2)}, u32[]{:S(2)}) collective-permute-start(bf16[16,16,128]{2,1,0:T(8,128)(2,1)S(1)} %get-tuple-element.25), channel_id=1, source_target_pairs={{0,6},{1,7},{2,0},{3,1},{4,2},{5,3},{6,4},{7,5},{8,14},{9,15},{10,... | collective-permute-start | bytes 196616 | tf_op jit(solution)/shard_map/ppermute | solution.py:336
  47.7 4.6 %collective-permute-start.8 = (bf16[16,16,128]{2,1,0:T(8,128)(2,1)S(1)}, bf16[16,16,128]{2,1,0:T(8,128)(2,1)S(1)}, u32[]{:S(2)}, u32[]{:S(2)}) collective-permute-start(bf16[16,16,128]{2,1,0:T(8,128)(2,1)S(1)} %get-tuple-element.25), channel_id=1, source_target_pairs={{0,4},{1,5},{2,6},{3,7},{4,0},{5,1},{6,2},{7,3},{8,12},{9,13},{10,... | collective-permute-start | bytes 196616 | tf_op jit(solution)/shard_map/ppermute | solution.py:336
  52.4 23.9 %collective-permute-start.10 = (bf16[64,16,128]{2,1,0:T(8,128)(2,1)S(1)}, bf16[64,16,128]{2,1,0:T(8,128)(2,1)S(1)}, u32[]{:S(2)}, u32[]{:S(2)}) collective-permute-start(bf16[64,16,128]{2,1,0:T(8,128)(2,1)S(1)} %get-tuple-element.17), channel_id=1, source_target_pairs={{0,1},{1,0},{2,3},{3,2},{4,5},{5,4},{6,7},{7,6},{8,9},{9,8},{10,11... | collective-permute-start | bytes 786440 | tf_op jit(solution)/shard_map/ppermute | solution.py:336
  62.3 0.7 copy-start
  76.3 0.9 copy-start.1

commit v2 on v0

v2 whole, which is shorter than its diff:
```python
import functools

import jax
import jax.numpy as jnp
import ml_dtypes
import numpy as np
from jax import lax
from jax.experimental import pallas as pl
from jax.experimental.pallas import tpu as pltpu
from jax.sharding import PartitionSpec as P

TD = 2048
HALF = 1024
TAPS = 64
CH = 128
NA = 16
NB = 8
SHAPE = (4, 4, 4, 2)
NN = (((1,), (0,)), ((), ()))
NT = (((1,), (1,)), ((), ()))
F32 = jnp.float32
BF16 = jnp.bfloat16


def bins(first, step, count):
    col = np.arange(count)
    rank = col // 128 * 8 + col % 128 // 16
    return 64 * (col % 16) + step * rank + first


def split_table(table):
    high = table.astype(ml_dtypes.bfloat16)
    low = (table - high.astype(np.float64)).astype(ml_dtypes.bfloat16)
    return np.stack([high, low])


def cot(num):
    return 1.0 / np.tan(np.pi * num / TD)


def wave(freq, times):
    ang = 2 * np.pi * (freq[None, :] * times % TD) / TD
    return np.cos(ang), -np.sin(ang)


@functools.cache
def tables():
    quads = [bins(0, 4, 256), bins(2, 4, 256)]
    odd = bins(1, 2, 512)
    even = np.concatenate(quads)
    time = np.arange(512)[:, None]
    dft = []
    for freq in quads:
        re, im = wave(freq, time)
        if freq[0] == 0:
            im[:, 0] = (-1.0) ** np.arange(512)
        dft.append(split_table(np.concatenate([re, im], 1)))
    fe, fo = even[:, None], odd[None, :]
    norm = 2.0 / HALF
    re_im = -0.5 * (cot(fe + fo) + cot(fo - fe)) * np.where(fe == 0, 0.5 * norm, norm)
    im_re = -0.5 * (cot(fe + fo) + cot(fe - fo)) * np.where(fe == 0, 0.0, norm)
    nyquist = -0.5 * (cot(HALF + fo) + cot(fo - HALF)) / HALF
    rows = np.arange(16)[:, None]
    tail = np.concatenate(
        wave(quads[0], rows) + wave(quads[1], rows) + tuple(-w for w in wave(odd, rows)), 1
    )
    both = np.concatenate([even, odd])[None, :]
    shift = 2 * np.pi * (both * np.arange(NB)[:, None] % TD) / TD
    coarse = 2 * np.pi * (both * (NB * np.arange(NA)[:, None] - 64) % TD) / TD
    place = np.zeros((TAPS, 640), np.float32)
    place[np.arange(TAPS), 128 - np.arange(TAPS)] = 1.0
    return dict(
        dft=np.stack(dft),
        mix=np.stack([split_table(re_im), split_table(im_re)]),
        nyquist=nyquist.astype(np.float32),
        tail=split_table(tail),
        shift=np.stack([np.cos(shift), np.sin(shift)]).astype(np.float32),
        coarse=(np.stack([np.cos(coarse), np.sin(coarse)], 1) / 32.0).astype(np.float32),
        place=place,
    )


PAIRS = [(128 * k, at, at + 256) for k, at in enumerate((0, 128, 512, 640))]
ODD_PAIRS = [(512 + 128 * k, 1024 + 128 * k, 1536 + 128 * k) for k in range(4)]
ALL_PAIRS = PAIRS + ODD_PAIRS


def split(values):
    high = values.astype(BF16)
    return high, (values - high.astype(F32)).astype(BF16)


def dot3(values, table, dims=NN):
    high, low = split(values) if not isinstance(values, tuple) else values
    dot = functools.partial(lax.dot_general, dimension_numbers=dims, preferred_element_type=F32)
    rows = high.shape[0]
    both = dot(jnp.concatenate([high, low], 0), table[0])
    return both[:rows] + (both[rows:] + dot(high, table[1]))


def filter_band(fir, place):
    taps = jnp.broadcast_to(fir, (8, TAPS))
    row = lax.dot_general(
        taps, place, NN, precision=lax.Precision.HIGHEST, preferred_element_type=F32
    )
    band = pltpu.roll(jnp.broadcast_to(row[:1], (128, 640)), 0, 1, stride=4, stride_axis=0)
    return split(band)


def decimate(ext, off, band, dec):
    width = ext.shape[1]
    raw = ext[...]
    shifted = raw
    for step in range(1, 4):
        shifted = jnp.where(off == step, pltpu.roll(raw, width - step, 1), shifted)
    high, low = split(shifted)
    for block in range(8):
        at = slice(512 * block, 512 * block + 640)
        dec[:, 128 * block : 128 * block + 128] = dot3((high[:, at], low[:, at]), band, NT)
    at = slice(4096, 4352)
    seam = dot3((high[:, at], low[:, at]), (band[0][:, :256], band[1][:, :256]), NT)
    return jnp.where(lax.axis_index("sec") == 0, seam, 0.0)


def even_bins(dec, dft, out):
    first, second = dec[:, :512], dec[:, 512:]
    for quad, folded in enumerate((first + second, first - second)):
        out[:, 512 * quad : 512 * quad + 512] = dot3(folded, (dft[quad, 0], dft[quad, 1]))


def pad_edges(ext):
    width = ext.shape[1]
    ext[:, :128] = jnp.zeros((ext.shape[0], 128), F32)
    ext[:, width - 128 :] = jnp.zeros((ext.shape[0], 128), F32)


def own_sources_kernel(
    source, offsets, strain, fir, place, dft_hbm, msg, near, ext, dec, even, dft, sems
):
    copies = []
    for slot in range(2):
        group = pl.multiple_of(source[slot] // 8 * 8, 8)
        copies.append(pltpu.make_async_copy(strain.at[pl.ds(group, 8)], near.at[slot], sems.at[slot]))
    fetch = pltpu.make_async_copy(dft_hbm, dft, sems.at[2])
    for copy in copies:
        copy.start()
    fetch.start()
    ext[...] = jnp.zeros(ext.shape, F32)
    band = filter_band(fir[...], place[...])
    row_id = lax.broadcasted_iota(jnp.int32, (8, 1), 0)
    off = jnp.where(row_id == 0, offsets[source[0]], offsets[source[1]])
    width = ext.shape[1]
    for slot in range(2):
        copies[slot].wait()
        ext[slot : slot + 1, 128 : width - 128] = near[slot, pl.ds(source[slot] % 8, 1), :]
    seam = decimate(ext, off, band, dec)
    fetch.wait()
    even_bins(dec, dft, even)
    for slot in range(2):
        values = even[slot : slot + 1, :]
        rows = [values[:, 128 * part : 128 * part + 128] for part in range(8)]
        rows += [seam[slot : slot + 1], jnp.zeros((7, 128), F32)]
        block = jnp.concatenate(rows, 0)
        for z in range(msg.shape[0] // 2):
            msg[msg.shape[0] // 2 * slot + z] = block


def prepare_kernel(
    strain, offset, fir, place, dft_hbm, e32_hbm, e16, tail_out, ext, dec, e32, dft, sems
):
    width = ext.shape[1]
    load = pltpu.make_async_copy(strain, ext.at[:, 128 : width - 128], sems.at[0])
    fetch = pltpu.make_async_copy(dft_hbm, dft, sems.at[1])
    load.start()
    fetch.start()
    pad_edges(ext)
    band = filter_band(fir[...], place[...])
    off = jnp.broadcast_to(offset[...].astype(F32), (CH, CH)).T[:, :1]
    load.wait()
    seam = decimate(ext, off, band, dec)
    tail_out[...] = seam
    fetch.wait()
    even_bins(dec, dft, e32)
    keep = pltpu.make_async_copy(e32, e32_hbm, sems.at[0])
    keep.start()
    for part in range(8):
        at = slice(128 * part, 128 * part + 128)
        e16[at, :] = e32[:, at].astype(BF16)
    e16[HALF : HALF + 16, :] = seam.T[:16].astype(BF16)
    keep.wait()


def whole_window(first, second, seam, mix, nyquist, tail):
    even = first + second
    diff = first - second
    real = jnp.concatenate([diff[:, :256], diff[:, 512:768]], 1)
    imag = jnp.concatenate([diff[:, 256:512], diff[:, 768:]], 1)
    added = dot3(seam[:, :16], (tail[0], tail[1]))
    even = even + added[:, :HALF]
    column = lax.broadcasted_iota(jnp.int32, even.shape, 1)
    even = jnp.where(column == 256, 0.0, even)
    ends = jnp.where(
        lax.broadcasted_iota(jnp.int32, (diff.shape[0], 128), 1) == 0,
        imag[:, :128] - real[:, :128],
        0.0,
    )
    total = ends
    for part in range(4):
        total = total + 2.0 * real[:, 128 * part : 128 * part + 128]
    start = jnp.sum(total, axis=1, keepdims=True) * (1.0 / HALF)
    odd_im = dot3(real, (mix[0, 0], mix[0, 1])) + imag[:, :1] * nyquist[...]
    odd_re = dot3(imag, (mix[1, 0], mix[1, 1])) + start
    spectrum = jnp.concatenate(
        [even, odd_re + added[:, HALF : HALF + 512], odd_im + added[:, HALF + 512 :]], 1
    )
    power = jnp.zeros((diff.shape[0], 128), F32)
    for part in range(16):
        piece = spectrum[:, 128 * part : 128 * part + 128]
        power = power + piece * piece
    for step in (16, 32, 64):
        power = power + pltpu.roll(power, step, 1)
    factor = 1.0 / jnp.sqrt(power * (1.0 / 128.0) + 1e-06)
    return spectrum * jnp.concatenate([factor] * 16, 1)


def source_kernel(parts, mix, nyquist, tail, out):
    def lines(half):
        rows = [parts[4 * half : 4 * half + 4, part, :] for part in range(8)]
        both = jnp.concatenate(rows, 1)
        return jnp.concatenate([both, both], 0)

    seam = parts[0:4, 8, :]
    white = whole_window(
        lines(0), lines(1), jnp.concatenate([seam, seam], 0), mix, nyquist, tail
    )
    rows = [
        white[k : k + 1, 128 * part : 128 * part + 128] for k in range(4) for part in range(16)
    ]
    block = jnp.concatenate(rows, 0).astype(BF16)
    for peer in range(out.shape[0]):
        out[peer] = block


def receiver_kernel(own_hbm, far, own_tail, mix, nyquist, tail, white, own, sem):
    load = pltpu.make_async_copy(own_hbm, own, sem)
    load.start()
    first_sec = lax.axis_index("sec") == 0
    got = jnp.concatenate(
        [far[128 * part : 128 * part + 128, :].astype(F32) for part in range(8)], 1
    )
    got_seam = jnp.concatenate(
        [far[HALF : HALF + 16, :].astype(F32), jnp.zeros((112, 128), F32)], 0
    ).T
    load.wait()
    mine = own[...]
    white[...] = whole_window(
        jnp.where(first_sec, mine, got),
        jnp.where(first_sec, got, mine),
        jnp.where(first_sec, own_tail[...], got_seam),
        mix,
        nyquist,
        tail,
    )


LINES = ((0, 64), (64, 64))
PART = 8
CHUNKS = NA // PART
SEND = 32


def turn_sources(chosen, shift, left, first, count, row):
    for two in range(count // 2):
        parts = [chosen[first + 2 * two + k].astype(F32) for k in range(2)]
        at = slice(row + 16 * two, row + 16 * two + 16)
        for col, re_at, im_at in ALL_PAIRS:
            cos = shift[0, :, col : col + 128]
            sin = shift[1, :, col : col + 128]
            up, low = re_at // 128, im_at // 128
            re = [jnp.broadcast_to(p[up : up + 1], (NB, 128)) for p in parts]
            im = [jnp.broadcast_to(p[low : low + 1], (NB, 128)) for p in parts]
            left[at, re_at : re_at + 128] = jnp.concatenate(
                [re[k] * cos + im[k] * sin for k in range(2)], 0
            ).astype(BF16)
            left[at, im_at : im_at + 128] = jnp.concatenate(
                [im[k] * cos - re[k] * sin for k in range(2)], 0
            ).astype(BF16)


def correlate_kernel(chosen, white, shift, coarse, out_hbm, *scratch):
    turned, rest = scratch[:CHUNKS], scratch[CHUNKS:]
    left, sums, (out, sems) = rest[:2], rest[2:4], rest[4:]

    def share(line, n):
        first, count = LINES[line]
        each = count // CHUNKS
        return first, n * each, each

    def turn(line, n):
        if line < len(LINES):
            first, at, count = share(line, n)
            turn_sources(chosen, shift, left[line % 2], first + at, count, at * NB)

    def build(n):
        if n >= CHUNKS:
            return
        for k in range(PART):
            a = n * PART + k
            at = slice(k * CH, k * CH + CH)
            for col, re_at, im_at in ALL_PAIRS:
                re = white[:, re_at : re_at + 128]
                im = white[:, im_at : im_at + 128]
                cos = coarse[a, 0:1, col : col + 128]
                sin = coarse[a, 1:2, col : col + 128]
                turned[n][at, re_at : re_at + 128] = (re * cos - im * sin).astype(BF16)
                turned[n][at, im_at : im_at + 128] = (re * sin + im * cos).astype(BF16)

    def product(line, n):
        rows = LINES[line][1] * NB
        total = lax.dot_general(
            left[line % 2][:rows], turned[n][...], NT, preferred_element_type=F32
        )
        for k in range(PART):
            sums[line % 2][n * PART + k, :rows] = total[:, CH * k : CH * k + CH]

    def finish(line, n):
        if line < 0:
            return
        first, start, count = share(line, n)
        for k in range(start, start + count):
            rel = first + k
            tile = sums[line % 2][:, k * NB : k * NB + NB, :].reshape(NA * NB, CH)
            out[rel // 32 * 32 + rel % 4 * 8 + rel % 32 // 4] = tile.T.astype(BF16)
            if (rel + 1) % SEND == 0:
                send(rel // SEND).start()

    def send(group):
        at = pl.ds(group * SEND, SEND)
        return pltpu.make_async_copy(out.at[at], out_hbm.at[at], sems.at[group])

    build(0)
    for n in range(CHUNKS):
        turn(0, n)
    for line in range(len(LINES)):
        for n in range(CHUNKS):
            product(line, n)
            if line == 0:
                build(n + 1)
            turn(line + 1, n)
            finish(line - 1, n)
    for n in range(CHUNKS):
        finish(len(LINES) - 1, n)
    for group in range(128 // SEND):
        send(group).wait()


def vmem(count):
    return [pl.BlockSpec(memory_space=pltpu.VMEM)] * count


SMEM = pl.BlockSpec(memory_space=pltpu.SMEM)
HBM = pl.BlockSpec(memory_space=pltpu.HBM)


def limit(mib):
    return pltpu.CompilerParams(vmem_limit_bytes=mib * 2**20)


def cost(mega_flops, mib):
    return pl.CostEstimate(flops=mega_flops * 10**6, bytes_accessed=mib * 2**20, transcendentals=0)


def own_sources(source, offset, strain, fir, tab):
    width = strain.shape[1] + 256
    return pl.pallas_call(
        own_sources_kernel,
        out_shape=jax.ShapeDtypeStruct((8, 16, 128), F32),
        in_specs=[SMEM, SMEM, HBM] + vmem(2) + [HBM],
        out_specs=vmem(1)[0],
        scratch_shapes=[
            pltpu.VMEM((2, 8, strain.shape[1]), F32),
            pltpu.VMEM((8, width), F32),
            pltpu.VMEM((8, HALF), F32),
            pltpu.VMEM((8, HALF), F32),
            pltpu.VMEM((2, 2, 512, 512), BF16),
            pltpu.SemaphoreType.DMA((3,)),
        ],
        compiler_params=limit(62),
        cost_estimate=cost(500, 3),
        name="own_sources",
    )(source, offset, strain, fir, tab["place"], tab["dft"])


def prepare(strain, offset, fir, tab):
    width = strain.shape[1] + 256
    shapes = [((CH, HALF), F32), ((HALF + 16, 128), BF16), ((CH, 128), F32)]
    return pl.pallas_call(
        prepare_kernel,
        out_shape=[jax.ShapeDtypeStruct(*s) for s in shapes],
        in_specs=[HBM] + vmem(3) + [HBM],
        out_specs=[HBM] + vmem(2),
        scratch_shapes=[
            pltpu.VMEM((CH, width), F32),
            pltpu.VMEM((CH, HALF), F32),
            pltpu.VMEM((CH, HALF), F32),
            pltpu.VMEM((2, 2, 512, 512), BF16),
            pltpu.SemaphoreType.DMA((2,)),
        ],
        compiler_params=limit(62),
        cost_estimate=cost(4000, 6),
        name="prepare",
    )(strain, offset, fir, tab["place"], tab["dft"])


def finish_sources(parts, peers, tab):
    return pl.pallas_call(
        source_kernel,
        out_shape=jax.ShapeDtypeStruct((peers, 64, 128), BF16),
        in_specs=vmem(4),
        out_specs=vmem(1)[0],
        compiler_params=limit(32),
        cost_estimate=cost(500, 3),
        name="finish_sources",
    )(parts, tab["mix"], tab["nyquist"], tab["tail"])


def finish_receivers(own, far, own_tail, tab):
    return pl.pallas_call(
        receiver_kernel,
        out_shape=jax.ShapeDtypeStruct((CH, TD), F32),
        in_specs=[HBM] + vmem(5),
        out_specs=vmem(1)[0],
        scratch_shapes=[pltpu.VMEM((CH, HALF), F32), pltpu.SemaphoreType.DMA],
        compiler_params=limit(32),
        cost_estimate=cost(3000, 6),
        name="finish_receivers",
    )(own, far, own_tail, tab["mix"], tab["nyquist"], tab["tail"])


def correlate(chosen, white, tab):
    longest = max(count for _, count in LINES)
    return pl.pallas_call(
        correlate_kernel,
        out_shape=jax.ShapeDtypeStruct((128, CH, 128), BF16),
        in_specs=vmem(4),
        out_specs=HBM,
        scratch_shapes=[pltpu.VMEM((PART * CH, TD), BF16)] * CHUNKS
        + [pltpu.VMEM((longest * NB, TD), BF16)] * 2
        + [pltpu.VMEM((NA, longest * NB, CH), F32)] * 2
        + [pltpu.VMEM((128, CH, 128), BF16), pltpu.SemaphoreType.DMA((128 // SEND,))],
        compiler_params=limit(44),
        cost_estimate=cost(9000, 13),
        name="correlate",
    )(chosen, white, tab["shift"], tab["coarse"])


def section_groups(size):
    y, z, x, core = SHAPE
    plane = x * core
    return [
        [s * size + (j * z + k) * plane + i for s in range(2) for k in range(z)]
        for j in range(y)
        for i in range(plane)
    ]


def plane_groups():
    y, z, x, core = SHAPE
    plane = x * core
    return [[(j * z + k) * plane + i for j in range(y) for i in range(plane)] for k in range(z)]


def per_device(strain, offset, fir_taps, source_channel):
    tab = tables()
    msg = own_sources(source_channel, offset, strain, fir_taps[None, :], tab)
    parts = lax.all_to_all(
        msg, ("sec", "rcv"), 0, 0, axis_index_groups=section_groups(lax.axis_size("rcv"))
    )
    strain, msg = lax.optimization_barrier((strain, msg))
    e32, e16, own_tail = prepare(strain, offset[None, :], fir_taps[None, :], tab)
    got16 = lax.ppermute(e16, "sec", [(0, 1), (1, 0)])
    groups = plane_groups()
    mine = finish_sources(parts, len(groups[0]), tab)
    chosen = lax.all_to_all(mine, "rcv", 0, 0, axis_index_groups=groups)
    white = finish_receivers(e32, got16, own_tail, tab)
    return correlate(chosen.reshape(128, 16, 128), white, tab)[None]


def solution(mesh):
    in_specs = (P("rcv", "sec"), P("rcv"), P(), P("rcv"))
    out_specs = P("sec", None, "rcv", None)
    return jax.shard_map(
        per_device, mesh=mesh, in_specs=in_specs, out_specs=out_specs, check_vma=False
    )
```

time: 892 us -> 63.1 us (0.07)
  other arithmetic: 325 us -> 0 us
  blocking collectives: 201 us -> 0 us
  local copies, waits for them, and re-layouts: 162 us -> 4.84 us
  matrix products: 137 us -> 0 us
  waiting for transfers between devices: 39.6 us -> 8.05 us
  Pallas kernels: 0 us -> 26.5 us
  starting transfers between devices: 9.65 us -> 23.1 us
  between operations: 13.6 us -> 0.26 us
    another operation x16 -> x0, other arithmetic: 305 us -> none  [the longest x8 163 us: cross_block(): jnp.stack([cross_re, cross_im], axis=2)]
    all_gather x2 -> x0, blocking collectives: 201 us -> none  [the longest x1 187 us: per_device(): lax.all_gather(chosen, 'rcv', axis=1, tiled=True)]
    dot_general x11 -> x0, matrix products: 137 us -> none  [the longest x8 91.2 us: per_block(): jnp.einsum('bfc,ft->bct', cross, table, preferred_element_type=jnp.float32)]
    convert_element_type x16 -> x0, local copies, waits for them, and re-layouts: 117 us -> none  [the longest x8 116 us: cross_block(): return jnp.stack([cross_re, cross_im], axis=2).reshape(block_size, row_co...]
    reduce_scatter x1 -> x0, waiting for transfers between devices: 39.6 us -> none  [per_device(): lax.psum_scatter(spectrum_block(jnp.arange(FREQ * lax.axis_size('sec'), d...]
    slice x13 -> x0, local copies, waits for them, and re-layouts: 34.4 us -> none  [the longest x4 33.6 us: decimate(): frames[:, phase, shift_pos:shift_pos + samples]]
    pallas_call x0 -> x5, Pallas kernels: none -> 26.5 us  [the longest x1 12.4 us: correlate(): pl.pallas_call(correlate_kernel, out_shape=jax.ShapeDtypeStruct((128, CH,...]
    all_to_all x0 -> x2, starting transfers between devices: none -> 17.6 us  [the longest x1 9.03 us: per_device(): lax.all_to_all(msg, ('sec', 'rcv'), 0, 0, axis_index_groups=section_group...]
  transfers between devices with their start and end apart: 2 -> 3, of which waited for: 1 -> 1; matrix products, arithmetic and copies ran while one was open for 1% -> 0% of each run, Pallas kernels for 0% -> 16%
where the time goes in v2:
time: 63.1 us; the launch traced here: 62.7 us
  Pallas kernels  26.5 us (42%)
  starting transfers between devices  23.1 us (37%)
  waiting for transfers between devices  8.05 us (13%)
  local copies, waits for them, and re-layouts  4.84 us (8%)
    pallas_call x1, Pallas kernels, correlate(): pl.pallas_call(correlate_kernel, out_shape=jax.ShapeDtypeStruct((128, CH,...  12.4 us
    all_to_all x1, starting transfers between devices, per_device(): lax.all_to_all(msg, ('sec', 'rcv'), 0, 0, axis_index_groups=section_group...  9.03 us
    all_to_all x1, starting transfers between devices, per_device(): chosen = lax.all_to_all(mine, 'rcv', 0, 0, axis_index_groups=groups)  8.6 us
    all_to_all x1, waiting for transfers between devices, per_device(): chosen = lax.all_to_all(mine, 'rcv', 0, 0, axis_index_groups=groups)  8.04 us
    pallas_call x1, Pallas kernels, prepare(): pl.pallas_call(prepare_kernel, out_shape=[jax.ShapeDtypeStruct(*s) for s...  6.91 us
    ppermute x1, starting transfers between devices, per_device(): got16 = lax.ppermute(e16, 'sec', [(0, 1), (1, 0)])  5.44 us
    unnamed x20, local copies, waits for them, and re-layouts  4.84 us
    pallas_call x1, Pallas kernels, own_sources(): pl.pallas_call(own_sources_kernel, out_shape=jax.ShapeDtypeStruct((8, 16,...  4.25 us
  transfers between devices with their start and end apart: 3, of which 1 were waited for; matrix products, arithmetic and copies ran while one was open for 0% of the time, Pallas kernels for 16%

profile of v2, /device:TPU:1, one launch (start us, length us, event | category | flops | bytes accessed | tf_op | source)
XLA Modules:
  0.0 62.7 jit_solution(15126887543863528769)
XLA Ops:
  0.0 4.2 %own_sources.1 = f32[8,16,128]{2,1,0:T(8,128)} custom-call(s32[2]{0:T(128)} %source.1, s32[128]{0:T(128)} %offsets.1, f32[128,4096]{1,0:T(8,128)} %strain.2, f32[1,64]{1,0:T(1,128)} %bitcast.6, f32[64,640]{1,0:T(8,128)} %constant.14.clone.place, bf16[2,2,512,512]{3,2,1,0:T(8,128)(2,1)} %constant.15.clone.dft_hbm), custom_call_target="tpu_custom_call" | custom-call | flops 500000000 | bytes 3145728 | tf_op jit(solution)/shard_map/own_sources/pallas_call | solution.py:375
  4.3 9.0 %all-to-all-start = ((f32[8,16,128]{2,1,0:T(8,128)}), f32[8,16,128]{2,1,0:T(8,128)S(1)}, u32[]{:S(2)}, u32[]{:S(2)}) async-start(f32[8,16,128]{2,1,0:T(8,128)} %own_sources.1), calls=%async_computation | async-start | bytes 131072 | tf_op jit(solution)/shard_map/all_to_all | solution.py:476
  13.3 0.0 copy-start.2
  13.3 0.0 copy-start.3
  13.3 6.9 %prepare.1 = (f32[128,1024]{1,0:T(8,128)}, bf16[1040,128]{1,0:T(8,128)(2,1)}, f32[128,128]{1,0:T(8,128)}) custom-call(f32[128,4096]{1,0:T(8,128)} %strain.2, s32[1,128]{1,0:T(1,128)} %bitcast.5, f32[1,64]{1,0:T(1,128)} %bitcast.7, f32[64,640]{1,0:T(8,128)} %constant.14.clone.place, bf16[2,2,512,512]{3,2,1,0:T(8,128)(2,1)} %constant.15.clone.dft_hbm), custom_call_target="tpu_custom_call" | custom-call | flops 4000000000 | bytes 6291456 | tf_op jit(solution)/shard_map/prepare/pallas_call | solution.py:397
  20.2 5.4 %collective-permute-start = (bf16[1040,128]{1,0:T(8,128)(2,1)}, bf16[1040,128]{1,0:T(8,128)(2,1)S(1)}, u32[]{:S(2)}, u32[]{:S(2)}) collective-permute-start(bf16[1040,128]{1,0:T(8,128)(2,1)} %get-tuple-element.11), channel_id=1, source_target_pairs={{0,128},{128,0},{1,129},{129,1},{2,130},{130,2},{3,131},{131,3},{4... | collective-permute-start | bytes 798728 | tf_op jit(solution)/shard_map/ppermute | solution.py:481
  25.7 0.0 all-to-all-done.parts
  25.7 0.0 copy-done.2
  25.7 0.0 copy-done.3
  25.7 0.0 copy-start
  25.7 1.6 %copy-done = bf16[2,2,512,512]{3,2,1,0:T(8,128)(2,1)S(1)} copy-done((bf16[2,2,512,512]{3,2,1,0:T(8,128)(2,1)S(1)}, bf16[2,2,512,512]{3,2,1,0:T(8,128)(2,1)}, u32[]{:S(2)}) %copy-start) | copy-done | bytes 2097176
  27.3 0.0 copy-start.1
  27.3 0.0 copy-start.9
  27.3 1.5 %finish_sources.1 = bf16[32,64,128]{2,1,0:T(8,128)(2,1)} custom-call(f32[8,16,128]{2,1,0:T(8,128)S(1)} %all-to-all-done.parts, bf16[2,2,512,512]{3,2,1,0:T(8,128)(2,1)S(1)} %copy-done, f32[1,512]{1,0:T(1,128)S(1)} %copy-done.3, bf16[2,16,2048]{2,1,0:T(8,128)(2,1)S(1)} %copy-done.2), custom_call_target="tpu_custom_call" | custom-call | flops 500000000 | bytes 3145728 | tf_op jit(solution)/shard_map/finish_sources/pallas_call | solution.py:416
  28.8 8.6 %all-to-all-start.1 = ((bf16[32,64,128]{2,1,0:T(8,128)(2,1)}), bf16[32,64,128]{2,1,0:T(8,128)(2,1)S(1)}, u32[]{:S(2)}, u32[]{:S(2)}) async-start(bf16[32,64,128]{2,1,0:T(8,128)(2,1)} %finish_sources.1), calls=%async_computation.1 | async-start | bytes 1048576 | tf_op jit(solution)/shard_map/all_to_all | solution.py:484
  37.4 0.0 collective-permute-done.far
  37.4 0.0 copy-done.1
  37.4 0.0 copy-done.9
  37.4 0.0 copy-start.8
  37.4 1.0 %copy-done.8 = f32[128,1024]{1,0:T(8,128)S(1)} copy-done((f32[128,1024]{1,0:T(8,128)S(1)}, f32[128,1024]{1,0:T(8,128)}, u32[]{:S(2)}) %copy-start.8) | copy-done | bytes 524312
  38.5 0.0 copy-start.4
  38.5 0.0 copy-start.5
  38.5 1.4 %finish_receivers.1.white = f32[128,2048]{1,0:T(8,128)S(1)} custom-call(f32[128,1024]{1,0:T(8,128)S(1)} %copy-done.8, bf16[1040,128]{1,0:T(8,128)(2,1)S(1)} %collective-permute-done.far, f32[128,128]{1,0:T(8,128)S(1)} %copy-done.9, bf16[2,2,512,512]{3,2,1,0:T(8,128)(2,1)S(1)} %copy-done.1, f32[1,512]{1,0:T(1,128)S(1)} %copy-done.3, ...), custom_call_target="tpu_custom_call" | custom-call | flops 3000000000 | bytes 6291456 | tf_op jit(solution)/shard_map/finish_receivers/pallas_call | solution.py:428
  39.9 0.0 copy-start.6
  39.9 1.0 %copy-done.6 = f32[128,2048]{1,0:T(8,128)} copy-done((f32[128,2048]{1,0:T(8,128)}, f32[128,2048]{1,0:T(8,128)S(1)}, u32[]{:S(2)}) %copy-start.6) | copy-done | bytes 1048600
  40.9 8.0 %all-to-all-done.1 = bf16[32,64,128]{2,1,0:T(8,128)(2,1)S(1)} async-done(((bf16[32,64,128]{2,1,0:T(8,128)(2,1)}), bf16[32,64,128]{2,1,0:T(8,128)(2,1)S(1)}, u32[]{:S(2)}, u32[]{:S(2)}) %all-to-all-start.1) | async-done | bytes 524320 | tf_op jit(solution)/shard_map/all_to_all | solution.py:484
  48.9 0.0 copy-done.4
  48.9 0.0 copy-done.5
  48.9 0.0 copy-start.7
  48.9 1.2 %copy-done.7 = f32[128,2048]{1,0:T(8,128)S(1)} copy-done((f32[128,2048]{1,0:T(8,128)S(1)}, f32[128,2048]{1,0:T(8,128)}, u32[]{:S(2)}) %copy-start.7) | copy-done | bytes 1048600
  50.2 12.4 %correlate.1 = bf16[128,128,128]{2,1,0:T(8,128)(2,1)} custom-call(bf16[128,16,128]{2,1,0:T(8,128)(2,1)S(1)} %bitcast.4, f32[128,2048]{1,0:T(8,128)S(1)} %copy-done.7, f32[2,8,1024]{2,1,0:T(8,128)S(1)} %copy-done.5, f32[16,2,1024]{2,1,0:T(2,128)S(1)} %copy-done.4), custom_call_target="tpu_custom_call" | custom-call | flops 8999999488 | bytes 13631488 | tf_op jit(solution)/shard_map/correlate/pallas_call | solution.py:442
Async XLA Ops:
  4.3 21.4 %all-to-all-start = ((f32[8,16,128]{2,1,0:T(8,128)}), f32[8,16,128]{2,1,0:T(8,128)S(1)}, u32[]{:S(2)}, u32[]{:S(2)}) async-start(f32[8,16,128]{2,1,0:T(8,128)} %own_sources.1), calls=%async_computation | async-start | bytes 131072 | tf_op jit(solution)/shard_map/all_to_all | solution.py:476
  13.3 12.4 %copy-start.2 = (bf16[2,16,2048]{2,1,0:T(8,128)(2,1)S(1)}, bf16[2,16,2048]{2,1,0:T(8,128)(2,1)}, u32[]{:S(2)}) copy-start(bf16[2,16,2048]{2,1,0:T(8,128)(2,1)} %constant.18.clone.tail) | copy-start | bytes 393220
  13.3 12.4 %copy-start.3 = (f32[1,512]{1,0:T(1,128)S(1)}, f32[1,512]{1,0:T(1,128)}, u32[]{:S(2)}) copy-start(f32[1,512]{1,0:T(1,128)} %constant.17.clone.nyquist) | copy-start | bytes 6148
  20.2 17.2 %collective-permute-start = (bf16[1040,128]{1,0:T(8,128)(2,1)}, bf16[1040,128]{1,0:T(8,128)(2,1)S(1)}, u32[]{:S(2)}, u32[]{:S(2)}) collective-permute-start(bf16[1040,128]{1,0:T(8,128)(2,1)} %get-tuple-element.11), channel_id=1, source_target_pairs={{0,128},{128,0},{1,129},{129,1},{2,130},{130,2},{3,131},{131,3},{4... | collective-permute-start | bytes 798728 | tf_op jit(solution)/shard_map/ppermute | solution.py:481
  25.7 1.6 %copy-start = (bf16[2,2,512,512]{3,2,1,0:T(8,128)(2,1)S(1)}, bf16[2,2,512,512]{3,2,1,0:T(8,128)(2,1)}, u32[]{:S(2)}) copy-start(bf16[2,2,512,512]{3,2,1,0:T(8,128)(2,1)} %constant.16.clone.mix) | copy-start | bytes 6291460
  27.3 10.2 %copy-start.1 = (bf16[2,2,512,512]{3,2,1,0:T(8,128)(2,1)S(1)}, bf16[2,2,512,512]{3,2,1,0:T(8,128)(2,1)}, u32[]{:S(2)}) copy-start(bf16[2,2,512,512]{3,2,1,0:T(8,128)(2,1)} %constant.16.clone.mix) | copy-start | bytes 6291460
  27.3 10.2 %copy-start.9 = (f32[128,128]{1,0:T(8,128)S(1)}, f32[128,128]{1,0:T(8,128)}, u32[]{:S(2)}) copy-start(f32[128,128]{1,0:T(8,128)} %get-tuple-element.12.own_tail) | copy-start | bytes 196612
  28.8 20.2 %all-to-all-start.1 = ((bf16[32,64,128]{2,1,0:T(8,128)(2,1)}), bf16[32,64,128]{2,1,0:T(8,128)(2,1)S(1)}, u32[]{:S(2)}, u32[]{:S(2)}) async-start(bf16[32,64,128]{2,1,0:T(8,128)(2,1)} %finish_sources.1), calls=%async_computation.1 | async-start | bytes 1048576 | tf_op jit(solution)/shard_map/all_to_all | solution.py:484
  37.4 1.0 %copy-start.8 = (f32[128,1024]{1,0:T(8,128)S(1)}, f32[128,1024]{1,0:T(8,128)}, u32[]{:S(2)}) copy-start(f32[128,1024]{1,0:T(8,128)} %get-tuple-element.10.own_hbm) | copy-start | bytes 1572868
  38.5 10.5 %copy-start.4 = (f32[16,2,1024]{2,1,0:T(2,128)S(1)}, f32[16,2,1024]{2,1,0:T(2,128)}, u32[]{:S(2)}) copy-start(f32[16,2,1024]{2,1,0:T(2,128)} %constant.20.clone.coarse) | copy-start | bytes 393220
  38.5 10.5 %copy-start.5 = (f32[2,8,1024]{2,1,0:T(8,128)S(1)}, f32[2,8,1024]{2,1,0:T(8,128)}, u32[]{:S(2)}) copy-start(f32[2,8,1024]{2,1,0:T(8,128)} %constant.19.clone.shift) | copy-start | bytes 196612
  39.9 1.0 %copy-start.6 = (f32[128,2048]{1,0:T(8,128)}, f32[128,2048]{1,0:T(8,128)S(1)}, u32[]{:S(2)}) copy-start(f32[128,2048]{1,0:T(8,128)S(1)} %finish_receivers.1.white) | copy-start | bytes 3145732
  48.9 1.2 %copy-start.7 = (f32[128,2048]{1,0:T(8,128)S(1)}, f32[128,2048]{1,0:T(8,128)}, u32[]{:S(2)}) copy-start(f32[128,2048]{1,0:T(8,128)} %copy-done.6) | copy-start | bytes 3145732

commit v3 on v2

v3 whole, which is shorter than its diff:
```python
import functools

import jax
import jax.numpy as jnp
import ml_dtypes
import numpy as np
from jax import lax
from jax.experimental import pallas as pl
from jax.experimental.pallas import tpu as pltpu
from jax.sharding import PartitionSpec as P

TD = 2048
HALF = 1024
TAPS = 64
CH = 128
NA = 16
NB = 8
SHAPE = (4, 4, 4, 2)
NN = (((1,), (0,)), ((), ()))
NT = (((1,), (1,)), ((), ()))
F32 = jnp.float32
BF16 = jnp.bfloat16


def bins(first, step, count):
    col = np.arange(count)
    rank = col // 128 * 8 + col % 128 // 16
    return 64 * (col % 16) + step * rank + first


def split_table(table):
    high = table.astype(ml_dtypes.bfloat16)
    low = (table - high.astype(np.float64)).astype(ml_dtypes.bfloat16)
    return np.stack([high, low])


def cot(num):
    return 1.0 / np.tan(np.pi * num / TD)


def wave(freq, times):
    ang = 2 * np.pi * (freq[None, :] * times % TD) / TD
    return np.cos(ang), -np.sin(ang)


@functools.cache
def tables():
    quads = [bins(0, 4, 256), bins(2, 4, 256)]
    odd = bins(1, 2, 512)
    even = np.concatenate(quads)
    time = np.arange(512)[:, None]
    dft = []
    for freq in quads:
        re, im = wave(freq, time)
        if freq[0] == 0:
            im[:, 0] = (-1.0) ** np.arange(512)
        dft.append(split_table(np.concatenate([re, im], 1)))
    fe, fo = even[:, None], odd[None, :]
    norm = 2.0 / HALF
    re_im = -0.5 * (cot(fe + fo) + cot(fo - fe)) * np.where(fe == 0, 0.5 * norm, norm)
    im_re = -0.5 * (cot(fe + fo) + cot(fe - fo)) * np.where(fe == 0, 0.0, norm)
    nyquist = -0.5 * (cot(HALF + fo) + cot(fo - HALF)) / HALF
    rows = np.arange(16)[:, None]
    tail = np.concatenate(
        wave(quads[0], rows) + wave(quads[1], rows) + tuple(-w for w in wave(odd, rows)), 1
    )
    both = np.concatenate([even, odd])[None, :]
    shift = 2 * np.pi * (both * np.arange(NB)[:, None] % TD) / TD
    coarse = 2 * np.pi * (both * (NB * np.arange(NA)[:, None] - 64) % TD) / TD
    return dict(
        dft=np.stack(dft),
        mix=np.stack([split_table(re_im), split_table(im_re)]),
        nyquist=nyquist.astype(np.float32),
        tail=split_table(tail),
        shift=np.stack([np.cos(shift), np.sin(shift)]).astype(np.float32),
        coarse=(np.stack([np.cos(coarse), np.sin(coarse)], 1) / 32.0).astype(np.float32),
    )


PAIRS = [(128 * k, at, at + 256) for k, at in enumerate((0, 128, 512, 640))]
ODD_PAIRS = [(512 + 128 * k, 1024 + 128 * k, 1536 + 128 * k) for k in range(4)]
ALL_PAIRS = PAIRS + ODD_PAIRS


def split(values):
    high = values.astype(BF16)
    return high, (values - high.astype(F32)).astype(BF16)


def dot3(values, table, dims=NN):
    high, low = split(values) if not isinstance(values, tuple) else values
    dot = functools.partial(lax.dot_general, dimension_numbers=dims, preferred_element_type=F32)
    rows = high.shape[0]
    both = dot(jnp.concatenate([high, low], 0), table[0])
    return both[:rows] + (both[rows:] + dot(high, table[1]))


COLS = 1024


def spectrum(even, diff, seam, mix, nyquist, tail):
    real = jnp.concatenate([diff[:, :256], diff[:, 512:768]], 1)
    imag = jnp.concatenate([diff[:, 256:512], diff[:, 768:]], 1)
    added = dot3(seam[:, :16], (tail[0], tail[1]))
    even = even + added[:, :HALF]
    column = lax.broadcasted_iota(jnp.int32, even.shape, 1)
    even = jnp.where(column == 256, 0.0, even)
    total = jnp.where(
        lax.broadcasted_iota(jnp.int32, (diff.shape[0], 128), 1) == 0,
        imag[:, :128] - real[:, :128],
        0.0,
    )
    for part in range(4):
        total = total + 2.0 * real[:, 128 * part : 128 * part + 128]
    start = jnp.sum(total, axis=1, keepdims=True) * (1.0 / HALF)
    odd_im = dot3(real, (mix[0, 0], mix[0, 1])) + imag[:, :1] * nyquist[...]
    odd_re = dot3(imag, (mix[1, 0], mix[1, 1])) + start
    return jnp.concatenate(
        [even, odd_re + added[:, HALF : HALF + 512], odd_im + added[:, HALF + 512 :]], 1
    )


def whiten(values):
    power = jnp.zeros((values.shape[0], 128), F32)
    for part in range(16):
        piece = values[:, 128 * part : 128 * part + 128]
        power = power + piece * piece
    for step in (16, 32, 64):
        power = power + pltpu.roll(power, step, 1)
    factor = 1.0 / jnp.sqrt(power * (1.0 / 128.0) + 1e-06)
    return values * jnp.concatenate([factor] * 16, 1)


def first_section():
    return lax.axis_index("sec") == 0


def prepare_kernel(
    source_hbm, strain, offset_hbm, fir_hbm, dft_hbm, mix_hbm, nyquist_hbm, tail_hbm,
    msg_hbm, e32_hbm, e16_hbm, seam_hbm,
    source, offset, fir, dft, mix, nyquist, tail, msg, e16, seam_out, ext, dec, e32, sems, more,
):
    width = ext.shape[1]
    loads = []
    for part in range(strain.shape[1] // COLS):
        at = pl.ds(part * COLS, COLS)
        to = pl.ds(128 + part * COLS, COLS)
        loads.append(pltpu.make_async_copy(strain.at[:, at], ext.at[:, to], sems.at[part]))
    small = [(fir_hbm, fir), (offset_hbm, offset)]
    later = [
        (dft_hbm.at[0], dft.at[0]), (dft_hbm.at[1], dft.at[1]), (mix_hbm, mix),
        (nyquist_hbm, nyquist), (tail_hbm, tail), (source_hbm, source),
    ]
    fetch = [pltpu.make_async_copy(*ends, more.at[k]) for k, ends in enumerate(small + later)]
    for copy in fetch[:2] + loads + fetch[7:]:
        copy.start()
    ext[:, :128] = jnp.zeros((CH, 128), F32)
    ext[:, width - 128 :] = jnp.zeros((CH, 128), F32)
    lane = lax.broadcasted_iota(jnp.int32, (TAPS, 640), 1)
    tap = lax.broadcasted_iota(jnp.int32, (TAPS, 640), 0)
    place = jnp.where(lane + tap == 128, 1.0, 0.0).astype(F32)
    fetch[0].wait()
    row = lax.dot_general(
        jnp.broadcast_to(fir[...], (8, TAPS)),
        place,
        NN,
        precision=lax.Precision.HIGHEST,
        preferred_element_type=F32,
    )
    band = pltpu.roll(jnp.broadcast_to(row[:1], (128, 640)), 0, 1, stride=4, stride_axis=0)
    band = split(band)
    fetch[1].wait()
    off = jnp.broadcast_to(offset[...].astype(F32), (CH, CH)).T[:, :1]

    def filtered(start, length):
        raw = ext[:, start : min(start + length + 128, width)]
        size = raw.shape[1]
        raw = jnp.where(off >= 2.0, pltpu.roll(raw, size - 2, 1), raw)
        raw = jnp.where((off == 1.0) | (off == 3.0), pltpu.roll(raw, size - 1, 1), raw)
        return dot3(raw[:, :length], (band[0][:, :length], band[1][:, :length]), NT)

    for part, load in enumerate(loads):
        load.wait()
        if part == 1:
            for copy in fetch[2:7]:
                copy.start()
        for block in range(max(2 * part - 1, 0), 2 * part + 1):
            dec[:, 128 * block : 128 * block + 128] = filtered(512 * block, 640)
    dec[:, HALF - 128 :] = filtered(3584, 640)
    seam = jnp.where(first_section(), filtered(4096, 256), 0.0)
    seam_out[...] = seam
    first, second = dec[:, :512], dec[:, 512:]
    for quad, folded in enumerate((first + second, first - second)):
        fetch[2 + quad].wait()
        e32[:, 512 * quad : 512 * quad + 512] = dot3(folded, (dft[quad, 0], dft[quad, 1]))
    for part in range(8):
        at = slice(128 * part, 128 * part + 128)
        e16[at, :] = e32[:, at].astype(BF16)
    e16[HALF : HALF + 16, :] = seam.T[:16].astype(BF16)
    sends = [
        pltpu.make_async_copy(e32, e32_hbm, sems.at[0]),
        pltpu.make_async_copy(e16, e16_hbm, sems.at[1]),
        pltpu.make_async_copy(seam_out, seam_hbm, sems.at[2]),
        pltpu.make_async_copy(msg, msg_hbm, sems.at[3]),
    ]
    for copy in sends[:3]:
        copy.start()
    for copy in fetch[4:]:
        copy.wait()
    ids = [source[0], source[1]]
    even = jnp.concatenate([e32[pl.ds(src, 1), :] for src in ids] * 4, 0)
    edge = jnp.concatenate([seam_out[pl.ds(src, 1), :] for src in ids] * 4, 0)
    sign = jnp.where(first_section(), 1.0, -1.0).astype(F32)
    share = spectrum(even, even * sign, edge, mix, nyquist, tail)
    peers = msg.shape[0] // 2
    for slot in range(2):
        block = jnp.concatenate(
            [share[slot : slot + 1, 128 * part : 128 * part + 128] for part in range(16)], 0
        )
        for peer in range(peers):
            msg[peers * slot + peer] = block
    sends[3].start()
    for copy in sends:
        copy.wait()


def source_kernel(parts, out):
    count = parts.shape[0] // 2
    lines = [parts[:count, part, :] + parts[count:, part, :] for part in range(16)]
    white = whiten(jnp.concatenate([jnp.concatenate(lines, 1)] * 2, 0))
    rows = [
        white[k : k + 1, 128 * part : 128 * part + 128] for k in range(count) for part in range(16)
    ]
    block = jnp.concatenate(rows, 0).astype(BF16)
    for peer in range(out.shape[0]):
        out[peer] = block


def receiver_kernel(own_hbm, far, own_seam, mix, nyquist, tail, white, own, sem):
    load = pltpu.make_async_copy(own_hbm, own, sem)
    load.start()
    got = jnp.concatenate(
        [far[128 * part : 128 * part + 128, :].astype(F32) for part in range(8)], 1
    )
    got_seam = jnp.concatenate(
        [far[HALF : HALF + 16, :].astype(F32), jnp.zeros((112, 128), F32)], 0
    ).T
    load.wait()
    mine = own[...]
    sign = jnp.where(first_section(), 1.0, -1.0).astype(F32)
    seam = jnp.where(first_section(), own_seam[...], got_seam)
    white[...] = whiten(spectrum(mine + got, (mine - got) * sign, seam, mix, nyquist, tail))


LINES = 2
COUNT = 64
PART = 8
CHUNKS = NA // PART
SEND = 16


def turn_sources(chosen, shift, left, first, count, row):
    for two in range(count // 2):
        parts = [chosen[first + 2 * two + k].astype(F32) for k in range(2)]
        at = slice(row + 16 * two, row + 16 * two + 16)
        for col, re_at, im_at in ALL_PAIRS:
            cos = shift[0, :, col : col + 128]
            sin = shift[1, :, col : col + 128]
            up, low = re_at // 128, im_at // 128
            re = [jnp.broadcast_to(p[up : up + 1], (NB, 128)) for p in parts]
            im = [jnp.broadcast_to(p[low : low + 1], (NB, 128)) for p in parts]
            left[at, re_at : re_at + 128] = jnp.concatenate(
                [re[k] * cos + im[k] * sin for k in range(2)], 0
            ).astype(BF16)
            left[at, im_at : im_at + 128] = jnp.concatenate(
                [im[k] * cos - re[k] * sin for k in range(2)], 0
            ).astype(BF16)


def correlate_kernel(near, far, white, shift, coarse, out_hbm, *scratch):
    turned, rest = scratch[:CHUNKS], scratch[CHUNKS:]
    left, sums, (out, sems) = rest[:2], rest[2:4], rest[4:]
    each = COUNT // CHUNKS
    core = lax.rem(lax.axis_index("rcv"), 2)

    def turn(line, n):
        if line < LINES:
            turn_sources((near, far)[line], shift, left[line], n * each, each, n * each * NB)

    def build(n):
        if n >= CHUNKS:
            return
        for k in range(PART):
            a = n * PART + k
            at = slice(k * CH, k * CH + CH)
            for col, re_at, im_at in ALL_PAIRS:
                re = white[:, re_at : re_at + 128]
                im = white[:, im_at : im_at + 128]
                cos = coarse[a, 0:1, col : col + 128]
                sin = coarse[a, 1:2, col : col + 128]
                turned[n][at, re_at : re_at + 128] = (re * cos - im * sin).astype(BF16)
                turned[n][at, im_at : im_at + 128] = (re * sin + im * cos).astype(BF16)

    def product(line, n):
        total = lax.dot_general(left[line][...], turned[n][...], NT, preferred_element_type=F32)
        for k in range(PART):
            sums[line][n * PART + k] = total[:, CH * k : CH * k + CH]

    def finish(line, n):
        if line < 0:
            return
        for k in range(n * each, n * each + each):
            tile = sums[line][:, k * NB : k * NB + NB, :].reshape(NA * NB, CH)
            out[line, k // 16 * 16 + k % 4 * 4 + k % 16 // 4] = tile.T.astype(BF16)
            if (k + 1) % SEND == 0:
                send(line, k // SEND).start()

    def send(line, group):
        at = pl.ds(group * SEND, SEND)
        to = core if line == 0 else 1 - core
        sem = sems.at[line * (COUNT // SEND) + group]
        return pltpu.make_async_copy(out.at[line, at], out_hbm.at[at, to], sem)

    for n in range(CHUNKS):
        turn(0, n)
    build(0)
    for line in range(LINES):
        for n in range(CHUNKS):
            product(line, n)
            if line == 0:
                build(n + 1)
            turn(line + 1, n)
            finish(line - 1, n)
    for n in range(CHUNKS):
        finish(LINES - 1, n)
    for line in range(LINES):
        for group in range(COUNT // SEND):
            send(line, group).wait()


def vmem(count):
    return [pl.BlockSpec(memory_space=pltpu.VMEM)] * count


SMEM = pl.BlockSpec(memory_space=pltpu.SMEM)
HBM = pl.BlockSpec(memory_space=pltpu.HBM)


def limit(mib):
    return pltpu.CompilerParams(vmem_limit_bytes=mib * 2**20)


def cost(mega_flops, mib):
    return pl.CostEstimate(flops=mega_flops * 10**6, bytes_accessed=mib * 2**20, transcendentals=0)


def prepare(source, strain, offset, fir, tab):
    width = strain.shape[1] + 256
    constants = [tab["dft"], tab["mix"], tab["nyquist"], tab["tail"]]
    shapes = [
        ((8, 16, 128), F32),
        ((CH, HALF), F32),
        ((HALF + 16, 128), BF16),
        ((CH, 128), F32),
    ]
    return pl.pallas_call(
        prepare_kernel,
        out_shape=[jax.ShapeDtypeStruct(*s) for s in shapes],
        in_specs=[HBM] * 8,
        out_specs=[HBM] * 4,
        scratch_shapes=[
            pltpu.SMEM(source.shape, jnp.int32),
            pltpu.VMEM(offset.shape, jnp.int32),
            pltpu.VMEM(fir.shape, F32),
        ]
        + [pltpu.VMEM(t.shape, t.dtype) for t in constants]
        + [
            pltpu.VMEM((8, 16, 128), F32),
            pltpu.VMEM((HALF + 16, 128), BF16),
            pltpu.VMEM((CH, 128), F32),
            pltpu.VMEM((CH, width), F32),
            pltpu.VMEM((CH, HALF), F32),
            pltpu.VMEM((CH, HALF), F32),
            pltpu.SemaphoreType.DMA((strain.shape[1] // COLS,)),
            pltpu.SemaphoreType.DMA((8,)),
        ],
        compiler_params=limit(63),
        cost_estimate=cost(4000, 6),
        name="prepare",
    )(source, strain, offset, fir, *constants)


def finish_sources(parts, peers):
    return pl.pallas_call(
        source_kernel,
        out_shape=jax.ShapeDtypeStruct((peers, 64, 128), BF16),
        in_specs=vmem(1),
        out_specs=vmem(1)[0],
        compiler_params=limit(32),
        cost_estimate=cost(40000, 3),
        name="finish_sources",
    )(parts)


def finish_receivers(own, far, own_tail, tab):
    return pl.pallas_call(
        receiver_kernel,
        out_shape=jax.ShapeDtypeStruct((CH, TD), F32),
        in_specs=[HBM] + vmem(5),
        out_specs=vmem(1)[0],
        scratch_shapes=[pltpu.VMEM((CH, HALF), F32), pltpu.SemaphoreType.DMA],
        compiler_params=limit(32),
        cost_estimate=cost(3000, 6),
        name="finish_receivers",
    )(own, far, own_tail, tab["mix"], tab["nyquist"], tab["tail"])


def correlate(near, far, white, tab):
    return pl.pallas_call(
        correlate_kernel,
        out_shape=jax.ShapeDtypeStruct((COUNT, 2, CH, 128), BF16),
        in_specs=vmem(5),
        out_specs=HBM,
        scratch_shapes=[pltpu.VMEM((PART * CH, TD), BF16)] * CHUNKS
        + [pltpu.VMEM((COUNT * NB, TD), BF16)] * LINES
        + [pltpu.VMEM((NA, COUNT * NB, CH), F32)] * LINES
        + [
            pltpu.VMEM((LINES, COUNT, CH, 128), BF16),
            pltpu.SemaphoreType.DMA((LINES * COUNT // SEND,)),
        ],
        compiler_params=limit(32),
        cost_estimate=cost(9000, 13),
        name="correlate",
    )(near, far, white, tab["shift"], tab["coarse"])


def section_groups(size):
    y, z, x, core = SHAPE
    plane = x * core
    return [
        [s * size + (j * z + k) * plane + i for s in range(2) for k in range(z)]
        for j in range(y)
        for i in range(plane)
    ]


def plane_groups():
    y, z, x, core = SHAPE
    return [
        [((j * z + k) * x + i) * core + c for j in range(y) for i in range(x)]
        for k in range(z)
        for c in range(core)
    ]


def per_device(strain, offset, fir_taps, source_channel):
    tab = tables()
    size = lax.axis_size("rcv")
    msg, e32, e16, own_seam = prepare(
        source_channel, strain, offset[None, :], fir_taps[None, :], tab
    )
    parts = lax.all_to_all(msg, ("sec", "rcv"), 0, 0, axis_index_groups=section_groups(size))
    got16 = lax.ppermute(e16, "sec", [(0, 1), (1, 0)])
    groups = plane_groups()
    mine = finish_sources(parts, len(groups[0]))
    near = lax.all_to_all(mine, "rcv", 0, 0, axis_index_groups=groups)
    far = lax.ppermute(near, "rcv", [(k, k + 1 - 2 * (k % 2)) for k in range(size)])
    white = finish_receivers(e32, got16, own_seam, tab)
    out = correlate(near.reshape(COUNT, 16, 128), far.reshape(COUNT, 16, 128), white, tab)
    return out.reshape(1, 2 * COUNT, CH, 128)


def solution(mesh):
    in_specs = (P("rcv", "sec"), P("rcv"), P(), P("rcv"))
    out_specs = P("sec", None, "rcv", None)
    return jax.shard_map(
        per_device, mesh=mesh, in_specs=in_specs, out_specs=out_specs, check_vma=False
    )
```

time: 63.1 us -> 55.2 us (0.87)
  blocking collectives: 0 us -> 14.3 us
  waiting for transfers between devices: 8.05 us -> 1.85 us
  Pallas kernels: 26.5 us -> 20.4 us
  starting transfers between devices: 23.1 us -> 18.2 us
  local copies, waits for them, and re-layouts: 4.84 us -> 0.04 us
    all_to_all x0 -> x1, blocking collectives: none -> 14.3 us  [per_device(): near = lax.all_to_all(mine, 'rcv', 0, 0, axis_index_groups=groups)]
    all_to_all x1 -> x0, starting transfers between devices: 8.6 us -> none  [per_device(): chosen = lax.all_to_all(mine, 'rcv', 0, 0, axis_index_groups=groups)]
    all_to_all x1 -> x0, waiting for transfers between devices: 8.04 us -> none  [per_device(): chosen = lax.all_to_all(mine, 'rcv', 0, 0, axis_index_groups=groups)]
    unnamed x20 -> x14, local copies, waits for them, and re-layouts: 4.84 us -> 0.04 us
    pallas_call x2 -> x1, Pallas kernels: 16.6 us -> 12.2 us  [correlate(): pl.pallas_call(correlate_kernel, out_shape=jax.ShapeDtypeStruct((COUNT, 2...]
    ppermute x0 -> x1, starting transfers between devices: none -> 3.69 us  [per_device(): lax.ppermute(near, 'rcv', [(k, k + 1 - 2 * (k % 2)) for k in range(size)])]
    all_to_all x1, waiting for transfers between devices: 0.01 us -> 1.85 us  [per_device(): lax.all_to_all(msg, ('sec', 'rcv'), 0, 0, axis_index_groups=section_group...]
    pallas_call x1, Pallas kernels: 1.52 us -> 0.3 us  [finish_sources(): pl.pallas_call(source_kernel, out_shape=jax.ShapeDtypeStruct((peers, 64,...]
  transfers between devices with their start and end apart: 3 -> 3, of which waited for: 1 -> 1; matrix products, arithmetic and copies ran while one was open for 0% -> 0% of each run, Pallas kernels for 16% -> 3%
where the time goes in v3:
time: 55.2 us; the launch traced here: 55 us
  Pallas kernels  20.4 us (37%)
  starting transfers between devices  18.2 us (33%)
  blocking collectives  14.3 us (26%)
  waiting for transfers between devices  1.85 us (3%)
    all_to_all x1, blocking collectives, per_device(): near = lax.all_to_all(mine, 'rcv', 0, 0, axis_index_groups=groups)  14.3 us
    pallas_call x1, Pallas kernels, correlate(): pl.pallas_call(correlate_kernel, out_shape=jax.ShapeDtypeStruct((COUNT, 2...  12.2 us
    all_to_all x1, starting transfers between devices, per_device(): lax.all_to_all(msg, ('sec', 'rcv'), 0, 0, axis_index_groups=section_group...  9.03 us
    pallas_call x1, Pallas kernels, prepare(): pl.pallas_call(prepare_kernel, out_shape=[jax.ShapeDtypeStruct(*s) for s...  6.45 us
    ppermute x1, starting transfers between devices, per_device(): got16 = lax.ppermute(e16, 'sec', [(0, 1), (1, 0)])  5.44 us
    ppermute x1, starting transfers between devices, per_device(): lax.ppermute(near, 'rcv', [(k, k + 1 - 2 * (k % 2)) for k in range(size)])  3.69 us
    all_to_all x1, waiting for transfers between devices, per_device(): lax.all_to_all(msg, ('sec', 'rcv'), 0, 0, axis_index_groups=section_group...  1.85 us
    pallas_call x1, Pallas kernels, finish_receivers(): pl.pallas_call(receiver_kernel, out_shape=jax.ShapeDtypeStruct((CH, TD),...  1.39 us
  transfers between devices with their start and end apart: 3, of which 1 were waited for; matrix products, arithmetic and copies ran while one was open for 0% of the time, Pallas kernels for 3%

profile of v3, /device:TPU:1, one launch (start us, length us, event | category | flops | bytes accessed | tf_op | source)
XLA Modules:
  0.0 55.0 jit_solution(13827350150737594149)
XLA Ops:
  0.0 6.5 %prepare.1 = (f32[8,16,128]{2,1,0:T(8,128)}, f32[128,1024]{1,0:T(8,128)}, bf16[1040,128]{1,0:T(8,128)(2,1)}, f32[128,128]{1,0:T(8,128)}) custom-call(s32[2]{0:T(128)} %source_hbm.1, f32[128,4096]{1,0:T(8,128)} %strain.1, s32[1,128]{1,0:T(1,128)} %bitcast.7, f32[1,64]{1,0:T(1,128)} %bitcast.8, bf16[2,2,512,512]{3,2,1,0:T(8,128)(2,1)} %constant.12.clone.dft_hbm, ...), custom_call_target="tpu_custom_call" | custom-call | flops 4000000000 | bytes 6291456 | tf_op jit(solution)/shard_map/prepare/pallas_call | solution.py:366
  6.5 9.0 %all-to-all-start = ((f32[8,16,128]{2,1,0:T(8,128)}), f32[8,16,128]{2,1,0:T(8,128)S(1)}, u32[]{:S(2)}, u32[]{:S(2)}) async-start(f32[8,16,128]{2,1,0:T(8,128)} %get-tuple-element.9), calls=%async_computation | async-start | bytes 131072 | tf_op jit(solution)/shard_map/all_to_all | solution.py:462
  15.5 0.0 copy-start
  15.5 0.0 copy-start.2
  15.5 0.0 copy-start.4
  15.5 0.0 copy-start.5
  15.5 0.0 copy-start.6
  15.5 5.4 %collective-permute-start.1 = (bf16[1040,128]{1,0:T(8,128)(2,1)}, bf16[1040,128]{1,0:T(8,128)(2,1)S(1)}, u32[]{:S(2)}, u32[]{:S(2)}) collective-permute-start(bf16[1040,128]{1,0:T(8,128)(2,1)} %get-tuple-element.11), channel_id=1, source_target_pairs={{0,128},{128,0},{1,129},{129,1},{2,130},{130,2},{3,131},{131,3},{4... | collective-permute-start | bytes 798728 | tf_op jit(solution)/shard_map/ppermute | solution.py:463
  21.0 1.8 %all-to-all-done.parts = f32[8,16,128]{2,1,0:T(8,128)S(1)} async-done(((f32[8,16,128]{2,1,0:T(8,128)}), f32[8,16,128]{2,1,0:T(8,128)S(1)}, u32[]{:S(2)}, u32[]{:S(2)}) %all-to-all-start) | async-done | bytes 65568 | tf_op jit(solution)/shard_map/all_to_all | solution.py:462
  22.8 0.3 finish_sources.1
  23.1 14.3 %all_to_all.10 = bf16[16,64,128]{2,1,0:T(8,128)(2,1)S(1)} all-to-all(bf16[16,64,128]{2,1,0:T(8,128)(2,1)S(1)} %finish_sources.1), channel_id=1, replica_groups={{0,2,4,6,32,34,36,38,64,66,68,70,96,98,100,102},{1,3,5,7,33,35,37,39,65..., dimensions={0} | all-to-all | bytes 524288 | tf_op jit(solution)/shard_map/all_to_all | solution.py:466
  37.4 3.7 %collective-permute-start = (bf16[16,64,128]{2,1,0:T(8,128)(2,1)S(1)}, bf16[16,64,128]{2,1,0:T(8,128)(2,1)S(1)}, u32[]{:S(2)}, u32[]{:S(2)}) collective-permute-start(bf16[16,64,128]{2,1,0:T(8,128)(2,1)S(1)} %all_to_all.10), channel_id=1, source_target_pairs={{0,1},{1,0},{2,3},{3,2},{4,5},{5,4},{6,7},{7,6},{8,9},{9,8},{10,11... | collective-permute-start | bytes 786440 | tf_op jit(solution)/shard_map/ppermute | solution.py:467
  41.1 0.0 collective-permute-done.1.far
  41.1 0.0 copy-done
  41.1 0.0 copy-done.2
  41.1 0.0 copy-done.4
  41.1 0.0 copy-done.5
  41.1 0.0 copy-done.6
  41.1 0.0 copy-start.1
  41.1 0.0 copy-start.3
  41.2 1.4 %finish_receivers.1.white = f32[128,2048]{1,0:T(8,128)S(1)} custom-call(f32[128,1024]{1,0:T(8,128)S(1)} %copy-done.5, bf16[1040,128]{1,0:T(8,128)(2,1)S(1)} %collective-permute-done.1.far, f32[128,128]{1,0:T(8,128)S(1)} %copy-done.6, bf16[2,2,512,512]{3,2,1,0:T(8,128)(2,1)S(1)} %copy-done, f32[1,512]{1,0:T(1,128)S(1)} %copy-done.4, ...), custom_call_target="tpu_custom_call" | custom-call | flops 3000000000 | bytes 6291456 | tf_op jit(solution)/shard_map/finish_receivers/pallas_call | solution.py:406
  42.6 0.0 collective-permute-done
  42.6 0.0 copy-done.1
  42.6 0.0 copy-done.3
  42.6 12.2 %correlate.1 = bf16[64,2,128,128]{3,2,1,0:T(8,128)(2,1)} custom-call(bf16[64,16,128]{2,1,0:T(8,128)(2,1)S(1)} %bitcast.5, bf16[64,16,128]{2,1,0:T(8,128)(2,1)S(1)} %bitcast.6, f32[128,2048]{1,0:T(8,128)S(1)} %finish_receivers.1.white, f32[2,8,1024]{2,1,0:T(8,128)S(1)} %copy-done.3, f32[16,2,1024]{2,1,0:T(2,128)S(1)} %copy-done.1), custom_call_target="tpu_custom_call" | custom-call | flops 8999999488 | bytes 13631488 | tf_op jit(solution)/shard_map/correlate/pallas_call | solution.py:419
Async XLA Ops:
  6.5 16.4 %all-to-all-start = ((f32[8,16,128]{2,1,0:T(8,128)}), f32[8,16,128]{2,1,0:T(8,128)S(1)}, u32[]{:S(2)}, u32[]{:S(2)}) async-start(f32[8,16,128]{2,1,0:T(8,128)} %get-tuple-element.9), calls=%async_computation | async-start | bytes 131072 | tf_op jit(solution)/shard_map/all_to_all | solution.py:462
  15.5 25.6 %copy-start = (bf16[2,2,512,512]{3,2,1,0:T(8,128)(2,1)S(1)}, bf16[2,2,512,512]{3,2,1,0:T(8,128)(2,1)}, u32[]{:S(2)}) copy-start(bf16[2,2,512,512]{3,2,1,0:T(8,128)(2,1)} %constant.13.clone.mix_hbm.mix) | copy-start | bytes 6291460
  15.5 25.6 %copy-start.2 = (bf16[2,16,2048]{2,1,0:T(8,128)(2,1)S(1)}, bf16[2,16,2048]{2,1,0:T(8,128)(2,1)}, u32[]{:S(2)}) copy-start(bf16[2,16,2048]{2,1,0:T(8,128)(2,1)} %constant.15.clone.tail_hbm.tail) | copy-start | bytes 393220
  15.5 25.6 %copy-start.4 = (f32[1,512]{1,0:T(1,128)S(1)}, f32[1,512]{1,0:T(1,128)}, u32[]{:S(2)}) copy-start(f32[1,512]{1,0:T(1,128)} %constant.14.clone.nyquist_hbm.nyquist) | copy-start | bytes 6148
  15.5 25.6 %copy-start.5 = (f32[128,1024]{1,0:T(8,128)S(1)}, f32[128,1024]{1,0:T(8,128)}, u32[]{:S(2)}) copy-start(f32[128,1024]{1,0:T(8,128)} %get-tuple-element.10.own_hbm) | copy-start | bytes 1572868
  15.5 25.6 %copy-start.6 = (f32[128,128]{1,0:T(8,128)S(1)}, f32[128,128]{1,0:T(8,128)}, u32[]{:S(2)}) copy-start(f32[128,128]{1,0:T(8,128)} %get-tuple-element.12.own_seam) | copy-start | bytes 196612
  15.5 25.6 %collective-permute-start.1 = (bf16[1040,128]{1,0:T(8,128)(2,1)}, bf16[1040,128]{1,0:T(8,128)(2,1)S(1)}, u32[]{:S(2)}, u32[]{:S(2)}) collective-permute-start(bf16[1040,128]{1,0:T(8,128)(2,1)} %get-tuple-element.11), channel_id=1, source_target_pairs={{0,128},{128,0},{1,129},{129,1},{2,130},{130,2},{3,131},{131,3},{4... | collective-permute-start | bytes 798728 | tf_op jit(solution)/shard_map/ppermute | solution.py:463
  37.4 5.2 %collective-permute-start = (bf16[16,64,128]{2,1,0:T(8,128)(2,1)S(1)}, bf16[16,64,128]{2,1,0:T(8,128)(2,1)S(1)}, u32[]{:S(2)}, u32[]{:S(2)}) collective-permute-start(bf16[16,64,128]{2,1,0:T(8,128)(2,1)S(1)} %all_to_all.10), channel_id=1, source_target_pairs={{0,1},{1,0},{2,3},{3,2},{4,5},{5,4},{6,7},{7,6},{8,9},{9,8},{10,11... | collective-permute-start | bytes 786440 | tf_op jit(solution)/shard_map/ppermute | solution.py:467
  41.1 1.4 %copy-start.1 = (f32[16,2,1024]{2,1,0:T(2,128)S(1)}, f32[16,2,1024]{2,1,0:T(2,128)}, u32[]{:S(2)}) copy-start(f32[16,2,1024]{2,1,0:T(2,128)} %constant.17.clone.coarse) | copy-start | bytes 393220
  41.1 1.4 %copy-start.3 = (f32[2,8,1024]{2,1,0:T(8,128)S(1)}, f32[2,8,1024]{2,1,0:T(8,128)}, u32[]{:S(2)}) copy-start(f32[2,8,1024]{2,1,0:T(8,128)} %constant.16.clone.shift) | copy-start | bytes 196612

commit v4 on v3

--- a/solution.py
+++ b/solution.py
@@ -13,8 +13,8 @@
 HALF = 1024
 TAPS = 64
 CH = 128
-NA = 16
-NB = 8
+NA = 8
+NB = 16
 SHAPE = (4, 4, 4, 2)
 NN = (((1,), (0,)), ((), ()))
 NT = (((1,), (1,)), ((), ()))
@@ -95,7 +95,7 @@
     return both[:rows] + (both[rows:] + dot(high, table[1]))
 
 
-COLS = 1024
+COLS = 2048
 
 
 def spectrum(even, diff, seam, mix, nyquist, tail):
@@ -152,7 +152,7 @@
         (nyquist_hbm, nyquist), (tail_hbm, tail), (source_hbm, source),
     ]
     fetch = [pltpu.make_async_copy(*ends, more.at[k]) for k, ends in enumerate(small + later)]
-    for copy in fetch[:2] + loads + fetch[7:]:
+    for copy in fetch[:2] + loads + fetch[2:4] + fetch[7:]:
         copy.start()
     ext[:, :128] = jnp.zeros((CH, 128), F32)
     ext[:, width - 128 :] = jnp.zeros((CH, 128), F32)
@@ -182,9 +182,9 @@
     for part, load in enumerate(loads):
         load.wait()
         if part == 1:
-            for copy in fetch[2:7]:
+            for copy in fetch[4:7]:
                 copy.start()
-        for block in range(max(2 * part - 1, 0), 2 * part + 1):
+        for block in range(max(4 * part - 1, 0), 4 * part + 3):
             dec[:, 128 * block : 128 * block + 128] = filtered(512 * block, 640)
     dec[:, HALF - 128 :] = filtered(3584, 640)
     seam = jnp.where(first_section(), filtered(4096, 256), 0.0)
@@ -252,40 +252,43 @@
     white[...] = whiten(spectrum(mine + got, (mine - got) * sign, seam, mix, nyquist, tail))
 
 
-LINES = 2
 COUNT = 64
-PART = 8
+LINE = 64
+LINES = 2 * COUNT // LINE
+PART = 4
 CHUNKS = NA // PART
-SEND = 16
+SEND = 8
 
 
 def turn_sources(chosen, shift, left, first, count, row):
-    for two in range(count // 2):
-        parts = [chosen[first + 2 * two + k].astype(F32) for k in range(2)]
-        at = slice(row + 16 * two, row + 16 * two + 16)
+    for k in range(count):
+        values = chosen[first + k].astype(F32)
+        at = slice(row + NB * k, row + NB * k + NB)
         for col, re_at, im_at in ALL_PAIRS:
             cos = shift[0, :, col : col + 128]
             sin = shift[1, :, col : col + 128]
             up, low = re_at // 128, im_at // 128
-            re = [jnp.broadcast_to(p[up : up + 1], (NB, 128)) for p in parts]
-            im = [jnp.broadcast_to(p[low : low + 1], (NB, 128)) for p in parts]
-            left[at, re_at : re_at + 128] = jnp.concatenate(
-                [re[k] * cos + im[k] * sin for k in range(2)], 0
-            ).astype(BF16)
-            left[at, im_at : im_at + 128] = jnp.concatenate(
-                [im[k] * cos - re[k] * sin for k in range(2)], 0
-            ).astype(BF16)
+            re = jnp.broadcast_to(values[up : up + 1], (NB, 128))
+            im = jnp.broadcast_to(values[low : low + 1], (NB, 128))
+            left[at, re_at : re_at + 128] = (re * cos + im * sin).astype(BF16)
+            left[at, im_at : im_at + 128] = (im * cos - re * sin).astype(BF16)
 
 
 def correlate_kernel(near, far, white, shift, coarse, out_hbm, *scratch):
     turned, rest = scratch[:CHUNKS], scratch[CHUNKS:]
     left, sums, (out, sems) = rest[:2], rest[2:4], rest[4:]
-    each = COUNT // CHUNKS
+    each = LINE // CHUNKS
     core = lax.rem(lax.axis_index("rcv"), 2)
+
+    def place(line):
+        return line * LINE // COUNT, line * LINE % COUNT
 
     def turn(line, n):
         if line < LINES:
-            turn_sources((near, far)[line], shift, left[line], n * each, each, n * each * NB)
+            side, first = place(line)
+            turn_sources(
+                (near, far)[side], shift, left[line % 2], first + n * each, each, n * each * NB
+            )
 
     def build(n):
         if n >= CHUNKS:
@@ -302,24 +305,28 @@
                 turned[n][at, im_at : im_at + 128] = (re * sin + im * cos).astype(BF16)
 
     def product(line, n):
-        total = lax.dot_general(left[line][...], turned[n][...], NT, preferred_element_type=F32)
+        total = lax.dot_general(
+            left[line % 2][...], turned[n][...], NT, preferred_element_type=F32
+        )
         for k in range(PART):
-            sums[line][n * PART + k] = total[:, CH * k : CH * k + CH]
+            sums[line % 2][n * PART + k] = total[:, CH * k : CH * k + CH]
 
     def finish(line, n):
         if line < 0:
             return
+        side, first = place(line)
         for k in range(n * each, n * each + each):
-            tile = sums[line][:, k * NB : k * NB + NB, :].reshape(NA * NB, CH)
-            out[line, k // 16 * 16 + k % 4 * 4 + k % 16 // 4] = tile.T.astype(BF16)
+            row = (k // 16 * 16 + k % 4 * 4 + k % 16 // 4) * NB
+            tile = sums[line % 2][:, row : row + NB, :].reshape(NA * NB, CH)
+            out[side, first + k] = tile.T.astype(BF16)
             if (k + 1) % SEND == 0:
-                send(line, k // SEND).start()
-
-    def send(line, group):
+                send(side, (first + k) // SEND).start()
+
+    def send(side, group):
         at = pl.ds(group * SEND, SEND)
-        to = core if line == 0 else 1 - core
-        sem = sems.at[line * (COUNT // SEND) + group]
-        return pltpu.make_async_copy(out.at[line, at], out_hbm.at[at, to], sem)
+        to = core if side == 0 else 1 - core
+        sem = sems.at[side * (COUNT // SEND) + group]
+        return pltpu.make_async_copy(out.at[side, at], out_hbm.at[at, to], sem)
 
     for n in range(CHUNKS):
         turn(0, n)
@@ -333,9 +340,9 @@
             finish(line - 1, n)
     for n in range(CHUNKS):
         finish(LINES - 1, n)
-    for line in range(LINES):
+    for side in range(2):
         for group in range(COUNT // SEND):
-            send(line, group).wait()
+            send(side, group).wait()
 
 
 def vmem(count):
@@ -381,7 +388,7 @@
             pltpu.VMEM((CH, width), F32),
             pltpu.VMEM((CH, HALF), F32),
             pltpu.VMEM((CH, HALF), F32),
-            pltpu.SemaphoreType.DMA((strain.shape[1] // COLS,)),
+            pltpu.SemaphoreType.DMA((4,)),
             pltpu.SemaphoreType.DMA((8,)),
         ],
         compiler_params=limit(63),
@@ -422,11 +429,11 @@
         in_specs=vmem(5),
         out_specs=HBM,
         scratch_shapes=[pltpu.VMEM((PART * CH, TD), BF16)] * CHUNKS
-        + [pltpu.VMEM((COUNT * NB, TD), BF16)] * LINES
-        + [pltpu.VMEM((NA, COUNT * NB, CH), F32)] * LINES
+        + [pltpu.VMEM((LINE * NB, TD), BF16)] * 2
+        + [pltpu.VMEM((NA, LINE * NB, CH), F32)] * 2
         + [
-            pltpu.VMEM((LINES, COUNT, CH, 128), BF16),
-            pltpu.SemaphoreType.DMA((LINES * COUNT // SEND,)),
+            pltpu.VMEM((2, COUNT, CH, 128), BF16),
+            pltpu.SemaphoreType.DMA((2 * COUNT // SEND,)),
         ],
         compiler_params=limit(32),
         cost_estimate=cost(9000, 13),

time: 55.2 us -> 53.8 us (0.975)
  Pallas kernels: 20.4 us -> 19 us
    pallas_call x1, Pallas kernels: 12.2 us -> 11.4 us  [correlate(): pl.pallas_call(correlate_kernel, out_shape=jax.ShapeDtypeStruct((COUNT, 2...]
where the time goes in v4:
time: 53.8 us; the launch traced here: 53.6 us
  Pallas kernels  19 us (35%)
  starting transfers between devices  18.1 us (34%)
  blocking collectives  14.2 us (26%)
  waiting for transfers between devices  1.86 us (3%)
    all_to_all x1, blocking collectives, per_device(): near = lax.all_to_all(mine, 'rcv', 0, 0, axis_index_groups=groups)  14.2 us
    pallas_call x1, Pallas kernels, correlate(): pl.pallas_call(correlate_kernel, out_shape=jax.ShapeDtypeStruct((COUNT, 2...  11.4 us
    all_to_all x1, starting transfers between devices, per_device(): lax.all_to_all(msg, ('sec', 'rcv'), 0, 0, axis_index_groups=section_group...  9.03 us
    pallas_call x1, Pallas kernels, prepare(): pl.pallas_call(prepare_kernel, out_shape=[jax.ShapeDtypeStruct(*s) for s...  5.9 us
    ppermute x1, starting transfers between devices, per_device(): got16 = lax.ppermute(e16, 'sec', [(0, 1), (1, 0)])  5.44 us
    ppermute x1, starting transfers between devices, per_device(): lax.ppermute(near, 'rcv', [(k, k + 1 - 2 * (k % 2)) for k in range(size)])  3.68 us
    all_to_all x1, waiting for transfers between devices, per_device(): lax.all_to_all(msg, ('sec', 'rcv'), 0, 0, axis_index_groups=section_group...  1.85 us
    pallas_call x1, Pallas kernels, finish_receivers(): pl.pallas_call(receiver_kernel, out_shape=jax.ShapeDtypeStruct((CH, TD),...  1.39 us
  transfers between devices with their start and end apart: 3, of which 1 were waited for; matrix products, arithmetic and copies ran while one was open for 0% of the time, Pallas kernels for 3%

profile of v4, /device:TPU:1, one launch (start us, length us, event | category | flops | bytes accessed | tf_op | source)
XLA Modules:
  0.0 53.6 jit_solution(9747879968785794819)
XLA Ops:
  0.0 5.9 %prepare.1 = (f32[8,16,128]{2,1,0:T(8,128)}, f32[128,1024]{1,0:T(8,128)}, bf16[1040,128]{1,0:T(8,128)(2,1)}, f32[128,128]{1,0:T(8,128)}) custom-call(s32[2]{0:T(128)} %source_hbm.1, f32[128,4096]{1,0:T(8,128)} %strain.1, s32[1,128]{1,0:T(1,128)} %bitcast.7, f32[1,64]{1,0:T(1,128)} %bitcast.8, bf16[2,2,512,512]{3,2,1,0:T(8,128)(2,1)} %constant.12.clone.dft_hbm, ...), custom_call_target="tpu_custom_call" | custom-call | flops 4000000000 | bytes 6291456 | tf_op jit(solution)/shard_map/prepare/pallas_call | solution.py:373
  5.9 9.0 %all-to-all-start = ((f32[8,16,128]{2,1,0:T(8,128)}), f32[8,16,128]{2,1,0:T(8,128)S(1)}, u32[]{:S(2)}, u32[]{:S(2)}) async-start(f32[8,16,128]{2,1,0:T(8,128)} %get-tuple-element.9), calls=%async_computation | async-start | bytes 131072 | tf_op jit(solution)/shard_map/all_to_all | solution.py:469
  14.9 0.0 copy-start
  14.9 0.0 copy-start.2
  15.0 0.0 copy-start.4
  15.0 0.0 copy-start.5
  15.0 0.0 copy-start.6
  15.0 5.4 %collective-permute-start.1 = (bf16[1040,128]{1,0:T(8,128)(2,1)}, bf16[1040,128]{1,0:T(8,128)(2,1)S(1)}, u32[]{:S(2)}, u32[]{:S(2)}) collective-permute-start(bf16[1040,128]{1,0:T(8,128)(2,1)} %get-tuple-element.11), channel_id=1, source_target_pairs={{0,128},{128,0},{1,129},{129,1},{2,130},{130,2},{3,131},{131,3},{4... | collective-permute-start | bytes 798728 | tf_op jit(solution)/shard_map/ppermute | solution.py:470
  20.4 1.9 %all-to-all-done.parts = f32[8,16,128]{2,1,0:T(8,128)S(1)} async-done(((f32[8,16,128]{2,1,0:T(8,128)}), f32[8,16,128]{2,1,0:T(8,128)S(1)}, u32[]{:S(2)}, u32[]{:S(2)}) %all-to-all-start) | async-done | bytes 65568 | tf_op jit(solution)/shard_map/all_to_all | solution.py:469
  22.3 0.3 finish_sources.1
  22.6 14.2 %all_to_all.10 = bf16[16,64,128]{2,1,0:T(8,128)(2,1)S(1)} all-to-all(bf16[16,64,128]{2,1,0:T(8,128)(2,1)S(1)} %finish_sources.1), channel_id=1, replica_groups={{0,2,4,6,32,34,36,38,64,66,68,70,96,98,100,102},{1,3,5,7,33,35,37,39,65..., dimensions={0} | all-to-all | bytes 524288 | tf_op jit(solution)/shard_map/all_to_all | solution.py:473
  36.8 3.7 %collective-permute-start = (bf16[16,64,128]{2,1,0:T(8,128)(2,1)S(1)}, bf16[16,64,128]{2,1,0:T(8,128)(2,1)S(1)}, u32[]{:S(2)}, u32[]{:S(2)}) collective-permute-start(bf16[16,64,128]{2,1,0:T(8,128)(2,1)S(1)} %all_to_all.10), channel_id=1, source_target_pairs={{0,1},{1,0},{2,3},{3,2},{4,5},{5,4},{6,7},{7,6},{8,9},{9,8},{10,11... | collective-permute-start | bytes 786440 | tf_op jit(solution)/shard_map/ppermute | solution.py:474
  40.5 0.0 collective-permute-done.1.far
  40.5 0.0 copy-done
  40.5 0.0 copy-done.2
  40.5 0.0 copy-done.4
  40.5 0.0 copy-done.5
  40.5 0.0 copy-done.6
  40.5 0.0 copy-start.1
  40.6 0.0 copy-start.3
  40.6 1.4 %finish_receivers.1.white = f32[128,2048]{1,0:T(8,128)S(1)} custom-call(f32[128,1024]{1,0:T(8,128)S(1)} %copy-done.5, bf16[1040,128]{1,0:T(8,128)(2,1)S(1)} %collective-permute-done.1.far, f32[128,128]{1,0:T(8,128)S(1)} %copy-done.6, bf16[2,2,512,512]{3,2,1,0:T(8,128)(2,1)S(1)} %copy-done, f32[1,512]{1,0:T(1,128)S(1)} %copy-done.4, ...), custom_call_target="tpu_custom_call" | custom-call | flops 3000000000 | bytes 6291456 | tf_op jit(solution)/shard_map/finish_receivers/pallas_call | solution.py:413
  42.0 0.0 collective-permute-done
  42.0 0.0 copy-done.1
  42.0 0.0 copy-done.3
  42.0 11.4 %correlate.1 = bf16[64,2,128,128]{3,2,1,0:T(8,128)(2,1)} custom-call(bf16[64,16,128]{2,1,0:T(8,128)(2,1)S(1)} %bitcast.5, bf16[64,16,128]{2,1,0:T(8,128)(2,1)S(1)} %bitcast.6, f32[128,2048]{1,0:T(8,128)S(1)} %finish_receivers.1.white, f32[2,16,1024]{2,1,0:T(8,128)S(1)} %copy-done.1, f32[8,2,1024]{2,1,0:T(2,128)S(1)} %copy-done.3), custom_call_target="tpu_custom_call" | custom-call | flops 8999999488 | bytes 13631488 | tf_op jit(solution)/shard_map/correlate/pallas_call | solution.py:426
Async XLA Ops:
  5.9 16.4 %all-to-all-start = ((f32[8,16,128]{2,1,0:T(8,128)}), f32[8,16,128]{2,1,0:T(8,128)S(1)}, u32[]{:S(2)}, u32[]{:S(2)}) async-start(f32[8,16,128]{2,1,0:T(8,128)} %get-tuple-element.9), calls=%async_computation | async-start | bytes 131072 | tf_op jit(solution)/shard_map/all_to_all | solution.py:469
  14.9 25.6 %copy-start = (bf16[2,2,512,512]{3,2,1,0:T(8,128)(2,1)S(1)}, bf16[2,2,512,512]{3,2,1,0:T(8,128)(2,1)}, u32[]{:S(2)}) copy-start(bf16[2,2,512,512]{3,2,1,0:T(8,128)(2,1)} %constant.13.clone.mix_hbm.mix) | copy-start | bytes 6291460
  14.9 25.6 %copy-start.2 = (bf16[2,16,2048]{2,1,0:T(8,128)(2,1)S(1)}, bf16[2,16,2048]{2,1,0:T(8,128)(2,1)}, u32[]{:S(2)}) copy-start(bf16[2,16,2048]{2,1,0:T(8,128)(2,1)} %constant.15.clone.tail_hbm.tail) | copy-start | bytes 393220
  15.0 25.6 %copy-start.4 = (f32[1,512]{1,0:T(1,128)S(1)}, f32[1,512]{1,0:T(1,128)}, u32[]{:S(2)}) copy-start(f32[1,512]{1,0:T(1,128)} %constant.14.clone.nyquist_hbm.nyquist) | copy-start | bytes 6148
  15.0 25.6 %copy-start.5 = (f32[128,1024]{1,0:T(8,128)S(1)}, f32[128,1024]{1,0:T(8,128)}, u32[]{:S(2)}) copy-start(f32[128,1024]{1,0:T(8,128)} %get-tuple-element.10.own_hbm) | copy-start | bytes 1572868
  15.0 25.6 %copy-start.6 = (f32[128,128]{1,0:T(8,128)S(1)}, f32[128,128]{1,0:T(8,128)}, u32[]{:S(2)}) copy-start(f32[128,128]{1,0:T(8,128)} %get-tuple-element.12.own_seam) | copy-start | bytes 196612
  15.0 25.5 %collective-permute-start.1 = (bf16[1040,128]{1,0:T(8,128)(2,1)}, bf16[1040,128]{1,0:T(8,128)(2,1)S(1)}, u32[]{:S(2)}, u32[]{:S(2)}) collective-permute-start(bf16[1040,128]{1,0:T(8,128)(2,1)} %get-tuple-element.11), channel_id=1, source_target_pairs={{0,128},{128,0},{1,129},{129,1},{2,130},{130,2},{3,131},{131,3},{4... | collective-permute-start | bytes 798728 | tf_op jit(solution)/shard_map/ppermute | solution.py:470
  36.8 5.2 %collective-permute-start = (bf16[16,64,128]{2,1,0:T(8,128)(2,1)S(1)}, bf16[16,64,128]{2,1,0:T(8,128)(2,1)S(1)}, u32[]{:S(2)}, u32[]{:S(2)}) collective-permute-start(bf16[16,64,128]{2,1,0:T(8,128)(2,1)S(1)} %all_to_all.10), channel_id=1, source_target_pairs={{0,1},{1,0},{2,3},{3,2},{4,5},{5,4},{6,7},{7,6},{8,9},{9,8},{10,11... | collective-permute-start | bytes 786440 | tf_op jit(solution)/shard_map/ppermute | solution.py:474
  40.5 1.4 %copy-start.1 = (f32[2,16,1024]{2,1,0:T(8,128)S(1)}, f32[2,16,1024]{2,1,0:T(8,128)}, u32[]{:S(2)}) copy-start(f32[2,16,1024]{2,1,0:T(8,128)} %constant.16.clone.shift) | copy-start | bytes 393220
  40.6 1.4 %copy-start.3 = (f32[8,2,1024]{2,1,0:T(2,128)S(1)}, f32[8,2,1024]{2,1,0:T(2,128)}, u32[]{:S(2)}) copy-start(f32[8,2,1024]{2,1,0:T(2,128)} %constant.17.clone.coarse) | copy-start | bytes 196612

commit v5 on v4

--- a/solution.py
+++ b/solution.py
@@ -145,14 +145,21 @@
     for part in range(strain.shape[1] // COLS):
         at = pl.ds(part * COLS, COLS)
         to = pl.ds(128 + part * COLS, COLS)
-        loads.append(pltpu.make_async_copy(strain.at[:, at], ext.at[:, to], sems.at[part]))
+        loads.append(
+            [
+                pltpu.make_async_copy(
+                    strain.at[pl.ds(64 * h, 64), at], ext.at[pl.ds(64 * h, 64), to], sems.at[2 * part + h]
+                )
+                for h in range(2)
+            ]
+        )
     small = [(fir_hbm, fir), (offset_hbm, offset)]
     later = [
         (dft_hbm.at[0], dft.at[0]), (dft_hbm.at[1], dft.at[1]), (mix_hbm, mix),
         (nyquist_hbm, nyquist), (tail_hbm, tail), (source_hbm, source),
     ]
     fetch = [pltpu.make_async_copy(*ends, more.at[k]) for k, ends in enumerate(small + later)]
-    for copy in fetch[:2] + loads + fetch[2:4] + fetch[7:]:
+    for copy in fetch[:2] + loads[0] + loads[1] + fetch[2:4] + fetch[7:]:
         copy.start()
     ext[:, :128] = jnp.zeros((CH, 128), F32)
     ext[:, width - 128 :] = jnp.zeros((CH, 128), F32)
@@ -180,7 +187,8 @@
         return dot3(raw[:, :length], (band[0][:, :length], band[1][:, :length]), NT)
 
     for part, load in enumerate(loads):
-        load.wait()
+        for copy in load:
+            copy.wait()
         if part == 1:
             for copy in fetch[4:7]:
                 copy.start()

time: 53.8 us -> 53.8 us (level)
  no operation moved by 1% of the time
where the time goes in v5:
time: 53.8 us; the launch traced here: 53.6 us
  Pallas kernels  19 us (35%)
  starting transfers between devices  18.2 us (34%)
  blocking collectives  14.3 us (27%)
  waiting for transfers between devices  1.85 us (3%)
    all_to_all x1, blocking collectives, per_device(): near = lax.all_to_all(mine, 'rcv', 0, 0, axis_index_groups=groups)  14.3 us
    pallas_call x1, Pallas kernels, correlate(): pl.pallas_call(correlate_kernel, out_shape=jax.ShapeDtypeStruct((COUNT, 2...  11.4 us
    all_to_all x1, starting transfers between devices, per_device(): lax.all_to_all(msg, ('sec', 'rcv'), 0, 0, axis_index_groups=section_group...  9.03 us
    pallas_call x1, Pallas kernels, prepare(): pl.pallas_call(prepare_kernel, out_shape=[jax.ShapeDtypeStruct(*s) for s...  5.87 us
    ppermute x1, starting transfers between devices, per_device(): got16 = lax.ppermute(e16, 'sec', [(0, 1), (1, 0)])  5.44 us
    ppermute x1, starting transfers between devices, per_device(): lax.ppermute(near, 'rcv', [(k, k + 1 - 2 * (k % 2)) for k in range(size)])  3.69 us
    all_to_all x1, waiting for transfers between devices, per_device(): lax.all_to_all(msg, ('sec', 'rcv'), 0, 0, axis_index_groups=section_group...  1.85 us
    pallas_call x1, Pallas kernels, finish_receivers(): pl.pallas_call(receiver_kernel, out_shape=jax.ShapeDtypeStruct((CH, TD),...  1.39 us
  transfers between devices with their start and end apart: 3, of which 1 were waited for; matrix products, arithmetic and copies ran while one was open for 0% of the time, Pallas kernels for 3%

profile of v5, /device:TPU:1, one launch (start us, length us, event | category | flops | bytes accessed | tf_op | source)
XLA Modules:
  0.0 53.6 jit_solution(11672771260296995034)
XLA Ops:
  0.0 5.9 %prepare.1 = (f32[8,16,128]{2,1,0:T(8,128)}, f32[128,1024]{1,0:T(8,128)}, bf16[1040,128]{1,0:T(8,128)(2,1)}, f32[128,128]{1,0:T(8,128)}) custom-call(s32[2]{0:T(128)} %source_hbm.1, f32[128,4096]{1,0:T(8,128)} %strain.1, s32[1,128]{1,0:T(1,128)} %bitcast.7, f32[1,64]{1,0:T(1,128)} %bitcast.8, bf16[2,2,512,512]{3,2,1,0:T(8,128)(2,1)} %constant.12.clone.dft_hbm, ...), custom_call_target="tpu_custom_call" | custom-call | flops 4000000000 | bytes 6291456 | tf_op jit(solution)/shard_map/prepare/pallas_call | solution.py:381
  5.9 9.0 %all-to-all-start = ((f32[8,16,128]{2,1,0:T(8,128)}), f32[8,16,128]{2,1,0:T(8,128)S(1)}, u32[]{:S(2)}, u32[]{:S(2)}) async-start(f32[8,16,128]{2,1,0:T(8,128)} %get-tuple-element.9), calls=%async_computation | async-start | bytes 131072 | tf_op jit(solution)/shard_map/all_to_all | solution.py:477
  14.9 0.0 copy-start
  14.9 0.0 copy-start.2
  14.9 0.0 copy-start.4
  14.9 0.0 copy-start.5
  15.0 0.0 copy-start.6
  15.0 5.4 %collective-permute-start.1 = (bf16[1040,128]{1,0:T(8,128)(2,1)}, bf16[1040,128]{1,0:T(8,128)(2,1)S(1)}, u32[]{:S(2)}, u32[]{:S(2)}) collective-permute-start(bf16[1040,128]{1,0:T(8,128)(2,1)} %get-tuple-element.11), channel_id=1, source_target_pairs={{0,128},{128,0},{1,129},{129,1},{2,130},{130,2},{3,131},{131,3},{4... | collective-permute-start | bytes 798728 | tf_op jit(solution)/shard_map/ppermute | solution.py:478
  20.4 1.8 %all-to-all-done.parts = f32[8,16,128]{2,1,0:T(8,128)S(1)} async-done(((f32[8,16,128]{2,1,0:T(8,128)}), f32[8,16,128]{2,1,0:T(8,128)S(1)}, u32[]{:S(2)}, u32[]{:S(2)}) %all-to-all-start) | async-done | bytes 65568 | tf_op jit(solution)/shard_map/all_to_all | solution.py:477
  22.2 0.3 finish_sources.1
  22.6 14.3 %all_to_all.10 = bf16[16,64,128]{2,1,0:T(8,128)(2,1)S(1)} all-to-all(bf16[16,64,128]{2,1,0:T(8,128)(2,1)S(1)} %finish_sources.1), channel_id=1, replica_groups={{0,2,4,6,32,34,36,38,64,66,68,70,96,98,100,102},{1,3,5,7,33,35,37,39,65..., dimensions={0} | all-to-all | bytes 524288 | tf_op jit(solution)/shard_map/all_to_all | solution.py:481
  36.8 3.7 %collective-permute-start = (bf16[16,64,128]{2,1,0:T(8,128)(2,1)S(1)}, bf16[16,64,128]{2,1,0:T(8,128)(2,1)S(1)}, u32[]{:S(2)}, u32[]{:S(2)}) collective-permute-start(bf16[16,64,128]{2,1,0:T(8,128)(2,1)S(1)} %all_to_all.10), channel_id=1, source_target_pairs={{0,1},{1,0},{2,3},{3,2},{4,5},{5,4},{6,7},{7,6},{8,9},{9,8},{10,11... | collective-permute-start | bytes 786440 | tf_op jit(solution)/shard_map/ppermute | solution.py:482
  40.5 0.0 collective-permute-done.1.far
  40.5 0.0 copy-done
  40.5 0.0 copy-done.2
  40.5 0.0 copy-done.4
  40.5 0.0 copy-done.5
  40.5 0.0 copy-done.6
  40.6 0.0 copy-start.1
  40.6 0.0 copy-start.3
  40.6 1.4 %finish_receivers.1.white = f32[128,2048]{1,0:T(8,128)S(1)} custom-call(f32[128,1024]{1,0:T(8,128)S(1)} %copy-done.5, bf16[1040,128]{1,0:T(8,128)(2,1)S(1)} %collective-permute-done.1.far, f32[128,128]{1,0:T(8,128)S(1)} %copy-done.6, bf16[2,2,512,512]{3,2,1,0:T(8,128)(2,1)S(1)} %copy-done, f32[1,512]{1,0:T(1,128)S(1)} %copy-done.4, ...), custom_call_target="tpu_custom_call" | custom-call | flops 3000000000 | bytes 6291456 | tf_op jit(solution)/shard_map/finish_receivers/pallas_call | solution.py:421
  42.0 0.0 collective-permute-done
  42.0 0.0 copy-done.1
  42.0 0.0 copy-done.3
  42.0 11.4 %correlate.1 = bf16[64,2,128,128]{3,2,1,0:T(8,128)(2,1)} custom-call(bf16[64,16,128]{2,1,0:T(8,128)(2,1)S(1)} %bitcast.5, bf16[64,16,128]{2,1,0:T(8,128)(2,1)S(1)} %bitcast.6, f32[128,2048]{1,0:T(8,128)S(1)} %finish_receivers.1.white, f32[2,16,1024]{2,1,0:T(8,128)S(1)} %copy-done.1, f32[8,2,1024]{2,1,0:T(2,128)S(1)} %copy-done.3), custom_call_target="tpu_custom_call" | custom-call | flops 8999999488 | bytes 13631488 | tf_op jit(solution)/shard_map/correlate/pallas_call | solution.py:434
Async XLA Ops:
  5.9 16.4 %all-to-all-start = ((f32[8,16,128]{2,1,0:T(8,128)}), f32[8,16,128]{2,1,0:T(8,128)S(1)}, u32[]{:S(2)}, u32[]{:S(2)}) async-start(f32[8,16,128]{2,1,0:T(8,128)} %get-tuple-element.9), calls=%async_computation | async-start | bytes 131072 | tf_op jit(solution)/shard_map/all_to_all | solution.py:477
  14.9 25.6 %copy-start = (bf16[2,2,512,512]{3,2,1,0:T(8,128)(2,1)S(1)}, bf16[2,2,512,512]{3,2,1,0:T(8,128)(2,1)}, u32[]{:S(2)}) copy-start(bf16[2,2,512,512]{3,2,1,0:T(8,128)(2,1)} %constant.13.clone.mix_hbm.mix) | copy-start | bytes 6291460
  14.9 25.6 %copy-start.2 = (bf16[2,16,2048]{2,1,0:T(8,128)(2,1)S(1)}, bf16[2,16,2048]{2,1,0:T(8,128)(2,1)}, u32[]{:S(2)}) copy-start(bf16[2,16,2048]{2,1,0:T(8,128)(2,1)} %constant.15.clone.tail_hbm.tail) | copy-start | bytes 393220
  14.9 25.6 %copy-start.4 = (f32[1,512]{1,0:T(1,128)S(1)}, f32[1,512]{1,0:T(1,128)}, u32[]{:S(2)}) copy-start(f32[1,512]{1,0:T(1,128)} %constant.14.clone.nyquist_hbm.nyquist) | copy-start | bytes 6148
  14.9 25.6 %copy-start.5 = (f32[128,1024]{1,0:T(8,128)S(1)}, f32[128,1024]{1,0:T(8,128)}, u32[]{:S(2)}) copy-start(f32[128,1024]{1,0:T(8,128)} %get-tuple-element.10.own_hbm) | copy-start | bytes 1572868
  15.0 25.6 %copy-start.6 = (f32[128,128]{1,0:T(8,128)S(1)}, f32[128,128]{1,0:T(8,128)}, u32[]{:S(2)}) copy-start(f32[128,128]{1,0:T(8,128)} %get-tuple-element.12.own_seam) | copy-start | bytes 196612
  15.0 25.6 %collective-permute-start.1 = (bf16[1040,128]{1,0:T(8,128)(2,1)}, bf16[1040,128]{1,0:T(8,128)(2,1)S(1)}, u32[]{:S(2)}, u32[]{:S(2)}) collective-permute-start(bf16[1040,128]{1,0:T(8,128)(2,1)} %get-tuple-element.11), channel_id=1, source_target_pairs={{0,128},{128,0},{1,129},{129,1},{2,130},{130,2},{3,131},{131,3},{4... | collective-permute-start | bytes 798728 | tf_op jit(solution)/shard_map/ppermute | solution.py:478
  36.8 5.2 %collective-permute-start = (bf16[16,64,128]{2,1,0:T(8,128)(2,1)S(1)}, bf16[16,64,128]{2,1,0:T(8,128)(2,1)S(1)}, u32[]{:S(2)}, u32[]{:S(2)}) collective-permute-start(bf16[16,64,128]{2,1,0:T(8,128)(2,1)S(1)} %all_to_all.10), channel_id=1, source_target_pairs={{0,1},{1,0},{2,3},{3,2},{4,5},{5,4},{6,7},{7,6},{8,9},{9,8},{10,11... | collective-permute-start | bytes 786440 | tf_op jit(solution)/shard_map/ppermute | solution.py:482
  40.6 1.4 %copy-start.1 = (f32[2,16,1024]{2,1,0:T(8,128)S(1)}, f32[2,16,1024]{2,1,0:T(8,128)}, u32[]{:S(2)}) copy-start(f32[2,16,1024]{2,1,0:T(8,128)} %constant.16.clone.shift) | copy-start | bytes 393220
  40.6 1.4 %copy-start.3 = (f32[8,2,1024]{2,1,0:T(2,128)S(1)}, f32[8,2,1024]{2,1,0:T(2,128)}, u32[]{:S(2)}) copy-start(f32[8,2,1024]{2,1,0:T(2,128)} %constant.17.clone.coarse) | copy-start | bytes 196612
